TPU v7x, 32 devices: a whole 2x2x4 slice. The times are simulated.
32 devices in a mesh: groups: 2 (over x), domain: 16 (over z, y, core).
Axes of the slice: x: 2, y: 2, z: 4, core: 2. Of those that a mesh axis runs over, the one named last changes fastest.
Arguments:
- patches: bfloat16 [512, 125, 256], P(('groups', 'domain')), parts along dimension 0, may hold values from -6 to 6
- destination: int32 [512], P(('groups', 'domain')), parts along dimension 0, may hold values from 0 to 15, as said below
- cotangent: bfloat16 [1024, 4, 512], P(('groups', 'domain')), parts along dimension 0, may hold values from -16 to 16
- conv_weight: bfloat16 [256, 27, 64], replicated, may hold values from -0.21875 to 0.21875
- conv_bias: float32 [64], replicated, may hold values from -3 to 3
- head_weight: float32 [64, 4], replicated, may hold values from -0.75 to 0.75
Outputs:
- grad_conv: float32 [512, 27, 64], P(('groups', 'domain')), parts along dimension 0
- grad_bias: float32 [128], P('groups'), parts along dimension 0
- grad_head: float32 [128, 4], P('groups'), parts along dimension 0
There are 2 independent parts, one for each index of `groups`. A program takes and returns all parts, laid end to end along the dimension named above; an argument that names none is the same for every part. Nothing has to cross between parts.
Inputs may be any that keep to these rules, and one draw needn't show every extreme that they name: `destination`: each trainer receives at most 32 patches and some trainer exactly 32; one owner sends at most 2 patch to one trainer and some pair reaches it; the patches of one trainer come from the owners as evenly as their number allows.
All inputs are finite; a program needn't handle non-finite values.
Results may differ from a plain program's by a relative error of at most 0.0029.
Values may be sent and summed in bfloat16 or wider, within the bound.
A program may use at most 64 MiB of HBM per device.

v0:
```python
import jax
import jax.numpy as jnp
import numpy as np
from jax import lax
from jax.sharding import PartitionSpec as P

C_IN = 256
C_OUT = 64
FIELDS = 4
TAPS = 27
PS = 4
PAD = 5
FINE = 512


def shift_plan():
    layout_plan = []
    for first_shift in (0, 1):
        for second_shift in (0, 1):
            for third_shift in (0, 1):
                per_axis = []
                for shift_bit in (first_shift, second_shift, third_shift):
                    per_axis.append([(1, 0)] if shift_bit == 1 else [(0, 1), (1, 2)])
                parity_ids = []
                tap_ids = []
                for first_pair in per_axis[0]:
                    for second_pair in per_axis[1]:
                        for third_pair in per_axis[2]:
                            parity_ids.append(
                                first_pair[0] * 4 + second_pair[0] * 2 + third_pair[0]
                            )
                            tap_ids.append(first_pair[1] * 9 + second_pair[1] * 3 + third_pair[1])
                layout_plan.append(((first_shift, second_shift, third_shift), parity_ids, tap_ids))
    return layout_plan


def local_terms(work_patches, work_cot, conv_weight, conv_bias, head_weight, layout_plan):
    slot_count = work_patches.shape[0]
    block_size = 8
    block_total = slot_count // block_size
    stacked_weights = [
        jnp.concatenate([conv_weight[:, tap_index, :] for tap_index in tap_ids], axis=1)
        for offsets, parity_ids, tap_ids in layout_plan
    ]
    patch_blocks = work_patches.reshape(block_total, block_size, PAD, PAD, PAD, C_IN)
    cot_blocks = work_cot.reshape(block_total, block_size, FIELDS, FINE)
    rows_here = block_size * PS**3

    def block_terms(running, inputs):
        bias_sum, head_sum = running
        padded_cube, cot_block = inputs
        hidden = jnp.zeros((rows_here, 8, C_OUT), jnp.float32)
        for (offsets, parity_ids, tap_ids), stacked in zip(layout_plan, stacked_weights):
            shifted = padded_cube[
                :,
                offsets[0] : offsets[0] + PS,
                offsets[1] : offsets[1] + PS,
                offsets[2] : offsets[2] + PS,
                :,
            ].reshape(rows_here, C_IN)
            product = jnp.dot(shifted, stacked, preferred_element_type=jnp.float32)
            hidden = hidden.at[:, np.array(parity_ids), :].add(
                product.reshape(rows_here, len(parity_ids), C_OUT)
            )
        hidden = hidden + conv_bias
        upstream_cot = cot_block.astype(jnp.float32).reshape(
            block_size, FIELDS, PS, 2, PS, 2, PS, 2
        )
        upstream_cot = upstream_cot.transpose(0, 2, 4, 6, 3, 5, 7, 1).reshape(rows_here, 8, FIELDS)
        sigmoid_h = jax.nn.sigmoid(hidden)
        active = hidden * sigmoid_h
        upstream = jnp.einsum(
            "rqf,of->rqo", upstream_cot, head_weight, precision=lax.Precision.HIGHEST
        )
        grad_hidden = upstream * sigmoid_h * (1.0 + hidden * (1.0 - sigmoid_h))
        bias_sum = bias_sum + jnp.sum(grad_hidden, axis=(0, 1))
        head_sum = head_sum + jnp.einsum(
            "rqo,rqf->of", active, upstream_cot, precision=lax.Precision.HIGHEST
        )
        return ((bias_sum, head_sum), grad_hidden.astype(jnp.bfloat16))

    initial = (jnp.zeros((C_OUT,), jnp.float32), jnp.zeros((C_OUT, FIELDS), jnp.float32))
    totals, grad_blocks = lax.scan(block_terms, initial, (patch_blocks, cot_blocks))
    return (totals, grad_blocks.reshape(slot_count * PS**3, 8, C_OUT))


def channel_grads(work_patches, grad_fine, layout_plan, row_count):
    slot_count = work_patches.shape[0]
    channels = work_patches
    channels = channels.reshape(slot_count, PAD, PAD, PAD, row_count)
    result = jnp.zeros((row_count, TAPS, C_OUT), jnp.float32)
    for offsets, parity_ids, tap_ids in layout_plan:
        shifted = channels[
            :,
            offsets[0] : offsets[0] + PS,
            offsets[1] : offsets[1] + PS,
            offsets[2] : offsets[2] + PS,
            :,
        ].reshape(slot_count * PS**3, row_count)
        chosen = grad_fine[:, np.array(parity_ids), :].reshape(
            slot_count * PS**3, len(parity_ids) * C_OUT
        )
        product = lax.dot_general(
            shifted, chosen, (((0,), (0,)), ((), ())), preferred_element_type=jnp.float32
        )
        result = result.at[:, np.array(tap_ids), :].add(
            product.reshape(row_count, len(parity_ids), C_OUT)
        )
    return result


def on_device(patches, destination, cotangent, conv_weight, conv_bias, head_weight):
    owners = lax.axis_size("domain")
    my_index = lax.axis_index("domain")
    own_rows = patches.shape[0]
    train_rows = cotangent.shape[0]
    per_pair = (train_rows + owners - 1) // owners
    slot_total = owners * per_pair
    layout_plan = shift_plan()
    listing = lax.all_gather(destination, "domain", axis=0, tiled=True)
    trainer_ids = jnp.arange(owners, dtype=jnp.int32)
    pair_counts = jnp.sum(
        (listing.reshape(owners, own_rows)[:, :, None] == trainer_ids[None, None, :]).astype(
            jnp.int32
        ),
        axis=1,
    )
    own_hits = (destination[:, None] == trainer_ids[None, :]).astype(jnp.int32)
    local_rank = jnp.sum(jnp.cumsum(own_hits, axis=0) * own_hits, axis=1) - 1
    incoming = jnp.sum(pair_counts * (trainer_ids == my_index).astype(jnp.int32)[None, :], axis=1)
    starts_in = jnp.cumsum(incoming) - incoming
    slot_rank = jnp.arange(per_pair, dtype=jnp.int32)
    slot_live = (slot_rank[None, :] < incoming[:, None]).reshape(slot_total)
    slot_place = (starts_in[:, None] + slot_rank[None, :]).reshape(slot_total)
    zero_value = jnp.zeros((), jnp.bfloat16)
    clipped = jnp.minimum(slot_place, train_rows - 1)
    outgoing = jnp.where(slot_live[:, None, None], cotangent[clipped], zero_value)
    arrived = lax.all_to_all(
        outgoing.reshape(owners, per_pair, FIELDS, FINE),
        "domain",
        split_axis=0,
        concat_axis=0,
        tiled=True,
    )
    arrived = arrived.reshape(slot_total, FIELDS, FINE)
    work_cot = arrived[destination * per_pair + local_rank]
    totals, grad_fine = local_terms(
        patches, work_cot, conv_weight, conv_bias, head_weight, layout_plan
    )
    grad_scale = float((owners * own_rows * PS**3) ** (-0.5))
    shard_rows = conv_weight.shape[0] // owners
    grad_conv = lax.psum_scatter(
        channel_grads(patches, grad_fine, layout_plan, shard_rows * lax.axis_size("domain")),
        "domain",
        scatter_dimension=0,
        tiled=True,
    )
    bias_total, head_total = lax.psum((totals[0], totals[1]), "domain")
    return (grad_conv * grad_scale, bias_total * grad_scale, head_total * grad_scale)


def solution(mesh):
    placed = (
        P(("groups", "domain"), None, None),
        P(("groups", "domain")),
        P(("groups", "domain"), None, None),
        P(),
        P(),
        P(),
    )
    return jax.shard_map(
        on_device,
        mesh=mesh,
        in_specs=placed,
        out_specs=(P(("groups", "domain"), None, None), P("groups"), P("groups", None)),
        check_vma=False,
    )
```

profile of v0, /device:TPU:0, one launch (start us, length us, event | category | flops | bytes accessed | tf_op | source)
XLA Modules:
  0.0 235.9 jit_solution(15943022215353345464)
XLA Ops:
  10.0 13.7 %all-reduce = s32[256]{0:T(256)S(1)} all-reduce(s32[256]{0:T(256)S(1)} %dynamic-update-slice.11), channel_id=1, replica_groups=mesh['groups'=2,'domain'=16] {'domain'}, use_global_device_ids=true, to_apply=%add | all-reduce | flops 256 | bytes 2048
  26.6 3.5 %all-to-all-start = ((bf16[16,2,4,512]{3,2,1,0:T(4,128)(2,1)}), bf16[16,2,4,512]{3,2,1,0:T(4,128)(2,1)S(1)}, u32[]{:S(2)}, u32[]{:S(2)}) async-start(bf16[16,2,4,512]{3,2,1,0:T(4,128)(2,1)} %broadcast_select_fusion.1), calls=%async_computation | async-start | bytes 262144 | tf_op jit(solution)/shard_map/all_to_all | solution.py:138
  30.9 1.9 fusion.20
  32.8 1.4 bitcast_dynamic-update-slice_fusion.8
  34.4 1.4 bitcast_dynamic-update-slice_fusion.7
  35.8 1.4 bitcast_dynamic-update-slice_fusion.6
  38.5 1.4 bitcast_dynamic-update-slice_fusion.4
  39.9 1.4 bitcast_dynamic-update-slice_fusion.3
  42.8 4.1 %fusion.19 = (bf16[16,4,4,4,256]{4,0,3,2,1:T(8,128)(2,1)S(1)}, bf16[16,4,4,4,256]{4,0,3,2,1:T(8,128)(2,1)S(1)}, bf16[16,4,4,4,256]{4,0,3,2,1:T(8,128)(2,1)S(1)},...) fusion(bf16[16,5,5,5,256]{4,0,3,2,1:T(8,128)(2,1)} %bitcast.36), kind=kLoop, calls=%fused_computation.114 | loop fusion | bytes 8388608 | tf_op jit(solution)/shard_map/slice | solution.py:93
  52.2 2.1 copy.157
  54.4 2.0 reshape.552
  56.3 2.1 copy.158
  58.4 1.9 reshape.555
  61.4 2.0 reshape.558
  69.4 1.4 bitcast_dynamic-update-slice_fusion.1
  72.1 51.3 %while.25 = (s32[]{:T(128)}, f32[64]{0:T(128)S(1)}, f32[64,4]{0,1:T(4,128)}, bf16[2,512,8,64]{1,3,2,0:T(8,128)(2,1)}, bf16[2,8,4,512]{3,2,1,0:T(4,128)(2,1)}, /*...) while((s32[]{:T(128)}, f32[64]{0:T(128)S(1)}, ...), condition=%wide.region_15.16_spmd.clone.clone.clone.clone, body=%wide.region_6.15_spmd.sunk.clone.clone.clone.clone.sunk | while | flops 483230272 | bytes 43551044 | solution.py:83
  73.3 1.7 fusion.104
  77.0 1.5 scatter_fusion
  89.2 3.7 %copy.173 = bf16[8,4,4,4,2,2,2,4]{3,2,1,0,7,6,5,4:T(4,128)(2,1)S(1)} copy(bf16[8,4,4,4,2,2,2,4]{0,6,3,5,2,4,1,7:T(2,128)(2,1)S(1)} %bitcast.309) | data formatting | bytes 65536 | tf_op jit(solution)/shard_map/while/body/eval_jaxpr/reshape | solution.py:69
  92.9 2.0 reshape.983
  99.0 1.7 fusion.104
  102.7 1.5 scatter_fusion
  114.9 3.7 %copy.173 = bf16[8,4,4,4,2,2,2,4]{3,2,1,0,7,6,5,4:T(4,128)(2,1)S(1)} copy(bf16[8,4,4,4,2,2,2,4]{0,6,3,5,2,4,1,7:T(2,128)(2,1)S(1)} %bitcast.309) | data formatting | bytes 65536 | tf_op jit(solution)/shard_map/while/body/eval_jaxpr/reshape | solution.py:69
  118.6 2.0 reshape.983
  126.2 1.5 gather_fusion.4
  129.1 1.4 gather_fusion.7
  131.9 2.4 %fusion.21 = f32[512,256]{1,0:T(8,128)} fusion(bf16[1024,512]{0,1:T(8,128)(2,1)S(1)} %bitcast.310, bf16[1024,256]{1,0:T(8,128)(2,1)} %reshape.552), kind=kOutput, calls=%fused_computation.116 | convolution fusion | flops 268435456 | bytes 2097152 | tf_op jit(solution)/shard_map/dot_general | solution.py:103
  141.4 1.7 scatter_fusion.8
  143.9 1.5 scatter_fusion.10
  148.8 4.4 %copy.148 = f32[256,27,64]{2,1,0:T(8,128)} copy(f32[256,27,64]{0,2,1:T(8,128)S(1)} %fusion.14) | data formatting | bytes 3538944 | tf_op jit(solution)/shard_map/scatter-add | solution.py:106
  153.9 33.9 %all-reduce.1 = (f32[64]{0:T(128)S(1)}, f32[64,4]{0,1:T(4,128)S(1)}) all-reduce(f32[64]{0:T(128)S(1)} %get-tuple-element.595, f32[64,4]{0,1:T(4,128)S(1)} %copy-done.49), channel_id=1, replica_groups=mesh['groups'=2,'domain'=16] {'domain'}, use_global_device_ids=true, to_apply=%region_25.26 | all-reduce | flops 320 | bytes 2560 | tf_op jit(solution)/shard_map/psum | solution.py:158
  188.9 38.4 %reduce-scatter.2.cloned.1.call-done = f32[16,27,64]{2,1,0:T(8,128)} async-done(((f32[256,27,64]{2,1,0:T(8,128)}), f32[16,27,64]{2,1,0:T(8,128)}) %reduce-scatter.2.cloned.1.call-update) | async-done | bytes 110608 | tf_op jit(solution)/shard_map/reduce_scatter | solution.py:152
  (285 shorter events, 75.4 us)
Async XLA Ops:
  7.2 18.0 %copy-start = (bf16[32,4,512]{2,1,0:T(4,128)(2,1)S(1)}, bf16[32,4,512]{2,1,0:T(4,128)(2,1)}, u32[]{:S(2)}) copy-start(bf16[32,4,512]{2,1,0:T(4,128)(2,1)} %param.62) | copy-start | bytes 393220
  7.2 27.0 %copy-start.46 = (s32[16]{0:T(128)S(1)}, s32[16]{0:T(128)}, u32[]{:S(2)}) copy-start(s32[16]{0:T(128)} %param.61) | copy-start | bytes 196
  26.6 44.2 %all-to-all-start = ((bf16[16,2,4,512]{3,2,1,0:T(4,128)(2,1)}), bf16[16,2,4,512]{3,2,1,0:T(4,128)(2,1)S(1)}, u32[]{:S(2)}, u32[]{:S(2)}) async-start(bf16[16,2,4,512]{3,2,1,0:T(4,128)(2,1)} %broadcast_select_fusion.1), calls=%async_computation | async-start | bytes 262144 | tf_op jit(solution)/shard_map/all_to_all | solution.py:138
  30.2 197.1 %reduce-scatter.2.cloned.1.call-start = ((), (), s32[]{:S(2)}) async-start(), calls=%async_computation.2 | async-start | bytes 4456448 | tf_op jit(solution)/shard_map/reduce_scatter | solution.py:152
  42.6 4.3 %copy-start.29 = (bf16[256,64]{0,1:T(8,128)(2,1)S(1)}, bf16[256,64]{0,1:T(8,128)(2,1)}, u32[]{:S(2)}) copy-start(bf16[256,64]{0,1:T(8,128)(2,1)} %get-tuple-element.992) | copy-start | bytes 98308
  42.7 4.3 %copy-start.30 = (bf16[256,64]{0,1:T(8,128)(2,1)S(1)}, bf16[256,64]{0,1:T(8,128)(2,1)}, u32[]{:S(2)}) copy-start(bf16[256,64]{0,1:T(8,128)(2,1)} %get-tuple-element.1009) | copy-start | bytes 98308
  42.7 4.9 %copy-start.42 = (s32[4]{0:T(128)S(1)}, s32[4]{0:T(128)}, u32[]{:S(2)}) copy-start(s32[4]{0:T(128)} %constant.193.clone) | copy-start | bytes 52
  42.7 4.9 %copy-start.43 = (s32[4]{0:T(128)S(1)}, s32[4]{0:T(128)}, u32[]{:S(2)}) copy-start(s32[4]{0:T(128)} %constant.194.clone) | copy-start | bytes 52
  42.7 5.5 %copy-start.39 = (s32[2]{0:T(128)S(1)}, s32[2]{0:T(128)}, u32[]{:S(2)}) copy-start(s32[2]{0:T(128)} %constant.195.clone) | copy-start | bytes 28
  42.7 5.5 %copy-start.44 = (s32[4]{0:T(128)S(1)}, s32[4]{0:T(128)}, u32[]{:S(2)}) copy-start(s32[4]{0:T(128)} %constant.196.clone) | copy-start | bytes 52
  42.7 6.1 %copy-start.40 = (s32[2]{0:T(128)S(1)}, s32[2]{0:T(128)}, u32[]{:S(2)}) copy-start(s32[2]{0:T(128)} %constant.197.clone) | copy-start | bytes 28
  42.7 6.1 %copy-start.41 = (s32[2]{0:T(128)S(1)}, s32[2]{0:T(128)}, u32[]{:S(2)}) copy-start(s32[2]{0:T(128)} %constant.198.clone) | copy-start | bytes 28
  42.7 6.7 %copy-start.35 = (bf16[256,64]{0,1:T(8,128)(2,1)S(1)}, bf16[256,64]{0,1:T(8,128)(2,1)}, u32[]{:S(2)}) copy-start(bf16[256,64]{0,1:T(8,128)(2,1)} %get-tuple-element.993) | copy-start | bytes 98308
  42.7 6.7 %copy-start.36 = (bf16[256,64]{0,1:T(8,128)(2,1)S(1)}, bf16[256,64]{0,1:T(8,128)(2,1)}, u32[]{:S(2)}) copy-start(bf16[256,64]{0,1:T(8,128)(2,1)} %get-tuple-element.994) | copy-start | bytes 98308
  42.7 6.6 %copy-start.37 = (bf16[256,64]{0,1:T(8,128)(2,1)S(1)}, bf16[256,64]{0,1:T(8,128)(2,1)}, u32[]{:S(2)}) copy-start(bf16[256,64]{0,1:T(8,128)(2,1)} %get-tuple-element.999) | copy-start | bytes 98308
  42.7 6.6 %copy-start.38 = (bf16[256,64]{0,1:T(8,128)(2,1)S(1)}, bf16[256,64]{0,1:T(8,128)(2,1)}, u32[]{:S(2)}) copy-start(bf16[256,64]{0,1:T(8,128)(2,1)} %get-tuple-element.1000) | copy-start | bytes 98308
  42.8 7.3 %copy-start.31 = (bf16[256,64]{0,1:T(8,128)(2,1)S(1)}, bf16[256,64]{0,1:T(8,128)(2,1)}, u32[]{:S(2)}) copy-start(bf16[256,64]{0,1:T(8,128)(2,1)} %get-tuple-element.995) | copy-start | bytes 98308
  42.8 7.3 %copy-start.32 = (bf16[256,64]{0,1:T(8,128)(2,1)S(1)}, bf16[256,64]{0,1:T(8,128)(2,1)}, u32[]{:S(2)}) copy-start(bf16[256,64]{0,1:T(8,128)(2,1)} %get-tuple-element.996) | copy-start | bytes 98308
  42.8 7.3 %copy-start.33 = (bf16[256,64]{0,1:T(8,128)(2,1)S(1)}, bf16[256,64]{0,1:T(8,128)(2,1)}, u32[]{:S(2)}) copy-start(bf16[256,64]{0,1:T(8,128)(2,1)} %get-tuple-element.997) | copy-start | bytes 98308
  42.8 7.3 %copy-start.34 = (bf16[256,64]{0,1:T(8,128)(2,1)S(1)}, bf16[256,64]{0,1:T(8,128)(2,1)}, u32[]{:S(2)}) copy-start(bf16[256,64]{0,1:T(8,128)(2,1)} %get-tuple-element.998) | copy-start | bytes 98308
  42.8 8.0 %copy-start.24 = (bf16[256,64]{0,1:T(8,128)(2,1)S(1)}, bf16[256,64]{0,1:T(8,128)(2,1)}, u32[]{:S(2)}) copy-start(bf16[256,64]{0,1:T(8,128)(2,1)} %get-tuple-element.1004) | copy-start | bytes 98308
  42.8 8.0 %copy-start.25 = (bf16[256,64]{0,1:T(8,128)(2,1)S(1)}, bf16[256,64]{0,1:T(8,128)(2,1)}, u32[]{:S(2)}) copy-start(bf16[256,64]{0,1:T(8,128)(2,1)} %get-tuple-element.1005) | copy-start | bytes 98308
  42.8 8.0 %copy-start.26 = (bf16[256,64]{0,1:T(8,128)(2,1)S(1)}, bf16[256,64]{0,1:T(8,128)(2,1)}, u32[]{:S(2)}) copy-start(bf16[256,64]{0,1:T(8,128)(2,1)} %get-tuple-element.1006) | copy-start | bytes 98308
  42.8 7.9 %copy-start.27 = (bf16[256,64]{0,1:T(8,128)(2,1)S(1)}, bf16[256,64]{0,1:T(8,128)(2,1)}, u32[]{:S(2)}) copy-start(bf16[256,64]{0,1:T(8,128)(2,1)} %get-tuple-element.1007) | copy-start | bytes 98308
  42.8 7.9 %copy-start.28 = (bf16[256,64]{0,1:T(8,128)(2,1)S(1)}, bf16[256,64]{0,1:T(8,128)(2,1)}, u32[]{:S(2)}) copy-start(bf16[256,64]{0,1:T(8,128)(2,1)} %get-tuple-element.1008) | copy-start | bytes 98308
  88.9 6.0 %copy-start.57 = (f32[64,4]{0,1:T(4,128)S(1)}, f32[64,4]{0,1:T(4,128)}, u32[]{:S(2)}) copy-start(f32[64,4]{0,1:T(4,128)} %get-tuple-element.1196) | copy-start | bytes 3076 | tf_op jit(solution)/shard_map/while
  88.9 6.0 %copy-start.58 = (f32[64]{0:T(128)S(1)}, f32[64]{0:T(128)}, u32[]{:S(2)}) copy-start(f32[64]{0:T(128)} %get-tuple-element.1206) | copy-start | bytes 772 | tf_op jit(solution)/shard_map/while
  114.6 6.0 %copy-start.57 = (f32[64,4]{0,1:T(4,128)S(1)}, f32[64,4]{0,1:T(4,128)}, u32[]{:S(2)}) copy-start(f32[64,4]{0,1:T(4,128)} %get-tuple-element.1196) | copy-start | bytes 3076 | tf_op jit(solution)/shard_map/while
  114.6 6.0 %copy-start.58 = (f32[64]{0:T(128)S(1)}, f32[64]{0:T(128)}, u32[]{:S(2)}) copy-start(f32[64]{0:T(128)} %get-tuple-element.1206) | copy-start | bytes 772 | tf_op jit(solution)/shard_map/while
  131.9 3.4 %copy-start.17 = (bf16[1024,256]{1,0:T(8,128)(2,1)S(1)}, bf16[1024,256]{1,0:T(8,128)(2,1)}, u32[]{:S(2)}) copy-start(bf16[1024,256]{1,0:T(8,128)(2,1)} %reshape.558) | copy-start | bytes 1572868
  141.4 4.1 %copy-start.9 = (f32[256,256]{1,0:T(8,128)S(1)}, f32[256,256]{1,0:T(8,128)}, u32[]{:S(2)}) copy-start(f32[256,256]{1,0:T(8,128)} %fusion.25) | copy-start | bytes 786436
  141.4 4.1 %copy-start.50 = (s32[4]{0:T(128)S(1)}, s32[4]{0:T(128)}, u32[]{:S(2)}) copy-start(s32[4]{0:T(128)} %constant.275) | copy-start | bytes 52
  (43 other events, 73.4 us)
Sparse Core Ops, SparseCore 0:
  153.4 73.8 reduce-scatter.1
where the time goes:
time: 238 us; the launch traced here: 236 us
  local copies, waits for them, and re-layouts  77.7 us (33%)
  blocking collectives  47.6 us (20%)
  waiting for transfers between devices  38.4 us (16%)
  other arithmetic  29.9 us (13%)
  matrix products  22.6 us (9%)
  between operations  15.3 us (6%)
  starting transfers between devices  3.55 us (1%)
    reduce_scatter x1, waiting for transfers between devices, on_device(): lax.psum_scatter(channel_grads(patches, grad_fine, layout_plan, shard_row...  38.4 us
    psum x1, blocking collectives, on_device(): bias_total, head_total = lax.psum((totals[0], totals[1]), 'domain')  33.9 us
    unnamed x110, local copies, waits for them, and re-layouts  20.8 us
    unnamed x1, blocking collectives  13.7 us
    scatter-add x14, other arithmetic, block_terms(): hidden.at[:, np.array(parity_ids), :]  13.5 us
    reshape x4, local copies, waits for them, and re-layouts, block_terms(): upstream_cot.transpose(0, 2, 4, 6, 3, 5, 7, 1).reshape(rows_here, 8, FIELDS)  11.3 us
    reshape x8, local copies, waits for them, and re-layouts, channel_grads(): shifted = channels[:, offsets[0]:offsets[0] + PS, offsets[1]:offsets[1] +...  10.5 us
    dot_general x16, matrix products, block_terms(): product = jnp.dot(shifted, stacked, preferred_element_type=jnp.float32)  9.47 us
  transfers between devices with their start and end apart: 2, of which 1 were waited for; matrix products, arithmetic and copies ran while one was open for 18% of the time, Pallas kernels for 0%

commit v1 on v0

v1 whole, which is shorter than its diff:
```python
import functools
import itertools

import jax
import jax.numpy as jnp
import numpy as np
from jax import lax
from jax.experimental import pallas as pl
from jax.experimental.pallas import tpu as pltpu
from jax.sharding import PartitionSpec as P

FIELDS = 4
TAPS = 27
PS = 4
PAD = 5
CELLS = PAD**3
CELLS_UP = 128
COARSE = PS**3
FINE = 8 * COARSE
BITS = list(itertools.product((0, 1), repeat=3))


def tap_of(shift, parity):
    tap = 0
    for s, q in zip(BITS[shift], BITS[parity]):
        if s == 1 and q == 0:
            return None
        tap = 3 * tap + (1 if q == 0 else (0 if s == 1 else 2))
    return tap


@functools.cache
def pick_tables():
    cells = list(itertools.product(range(PS), repeat=3))
    shifts = np.zeros((8, 2, COARSE, 2, CELLS_UP), np.float32)
    fine = np.zeros((8, COARSE, FINE), np.float32)
    for b, (b1, b2, b3) in enumerate(BITS):
        for j, (j1, j2, j3) in enumerate(cells):
            cell = (j1 + b1) * PAD * PAD + (j2 + b2) * PAD + j3 + b3
            for half in range(2):
                shifts[b, half, j, half, cell] = 1
            fine[b, j, (2 * j1 + b1) * 4 * PS * PS + (2 * j2 + b2) * 2 * PS + 2 * j3 + b3] = 1
    shifts = shifts.reshape(16 * COARSE, 2 * CELLS_UP)
    return shifts, np.ascontiguousarray(shifts.T), fine.reshape(FINE, FINE)


def dot(a, b, dims=((1,), (0,))):
    return lax.dot_general(a, b, (dims, ((), ())), preferred_element_type=jnp.float32)


def layer_kernel(
    patch_ref, cot_ref, w_ref, bias_ref, head_ref, pick_ref, pick_t_ref, fine_ref,
    part_ref, small_ref,
    cells, wide, turned, grads, view, head_big, head_sum, bias_sum,
):
    slots = patch_ref.shape[0]
    c_in = patch_ref.shape[2]
    c_out = w_ref.shape[2]
    half = 4 * c_out
    group = slots * FIELDS
    quad = 4 * group
    bf = jnp.bfloat16

    cells[...] = jnp.zeros_like(cells)
    for p in range(slots):
        cells[p * CELLS_UP : p * CELLS_UP + CELLS, :] = patch_ref[p]
    wide[...] = jnp.zeros_like(wide)
    for s in range(8):
        for q in range(8):
            tap = tap_of(s, q)
            if tap is not None:
                wide[s * c_in : (s + 1) * c_in, q * c_out : (q + 1) * c_out] = w_ref[tap]

    moved = dot(fine_ref[...], cot_ref[...], ((1,), (1,))).astype(bf)
    for q in range(8):
        view[:, q * group : (q + 1) * group] = moved[q * COARSE : (q + 1) * COARSE]

    row = lax.broadcasted_iota(jnp.int32, (quad, half), 0)
    col = lax.broadcasted_iota(jnp.int32, (quad, half), 1)
    same = row // group == col // c_out
    spread = jnp.zeros((quad, half), jnp.float32)
    for f in range(FIELDS):
        spread = jnp.where(same & (row % FIELDS == f), head_ref[f : f + 1, :], spread)
    for t in range(3):
        term = spread.astype(bf)
        head_big[t * quad : (t + 1) * quad, :] = term
        spread = spread - term.astype(jnp.float32)

    head_sum[...] = jnp.zeros_like(head_sum)
    bias_sum[...] = jnp.zeros_like(bias_sum)
    lane_slot = lax.broadcasted_iota(jnp.int32, (2 * COARSE, 2 * quad), 1) % group // FIELDS
    row_slot = lax.broadcasted_iota(jnp.int32, (2 * COARSE, 2 * quad), 0) // COARSE

    @pl.loop(0, slots // 2)
    def _(pair):
        rows = pl.ds(pl.multiple_of(pair * 2 * COARSE, 2 * COARSE), 2 * COARSE)
        both = cells[pl.ds(pl.multiple_of(pair * 2 * CELLS_UP, 2 * CELLS_UP), 2 * CELLS_UP), :]
        shifted = dot(pick_ref[...], both).astype(bf)
        turn = dot(both, pick_t_ref[...], ((0,), (0,))).astype(bf)
        for s in range(8):
            turned[s, :, rows] = turn[:, s * 2 * COARSE : (s + 1) * 2 * COARSE]
        beside = jnp.concatenate(
            [shifted[s * 2 * COARSE : (s + 1) * 2 * COARSE] for s in range(8)], axis=1
        )
        here = view[...].astype(jnp.float32)
        here = jnp.concatenate([here, here], axis=0)
        here = jnp.where(lane_slot == row_slot + 2 * pair, here, 0.0).astype(bf)
        for h in range(2):
            lanes = slice(h * half, (h + 1) * half)
            deep = (4 + 4 * h) * c_in
            hidden = dot(beside[:, :deep], wide[:deep, lanes]) + bias_ref[:, lanes]
            mine = here[:, h * quad : (h + 1) * quad]
            upstream = dot(jnp.concatenate([mine] * 3, axis=1), head_big[...])
            gate = jax.nn.sigmoid(hidden)
            active = hidden * gate
            grad = upstream * gate * (1.0 + hidden * (1.0 - gate))
            grads[rows, lanes] = grad.astype(bf)
            bias_sum[:, lanes] += jnp.sum(grad, axis=0, keepdims=True)
            top = active.astype(bf)
            rest = (active - top.astype(jnp.float32)).astype(bf)
            head_sum[...] += dot(mine, jnp.concatenate([top, rest], axis=1), ((0,), (0,)))

    for s in range(8):
        for h in range(2):
            if s >= 4 and h == 0:
                continue
            block = dot(turned[s], grads[:, h * half : (h + 1) * half]).astype(bf)
            for r in range(4):
                tap = tap_of(s, 4 * h + r)
                if tap is not None:
                    part_ref[:, tap * c_out : (tap + 1) * c_out] = block[:, r * c_out : (r + 1) * c_out]

    small_ref[...] = jnp.zeros_like(small_ref)
    small_ref[0:1, :] = bias_sum[...]
    row = lax.broadcasted_iota(jnp.int32, (quad, 2 * half), 0)
    col = lax.broadcasted_iota(jnp.int32, (quad, 2 * half), 1)
    kept = jnp.where(row // group == col % half // c_out, head_sum[...], 0.0)
    for f in range(FIELDS):
        small_ref[4 + f : 5 + f, :] = jnp.sum(
            jnp.where(row % FIELDS == f, kept, 0.0), axis=0, keepdims=True
        )


def layer(patches, work_cot, conv_weight, conv_bias, head_weight):
    slots, _, c_in = patches.shape
    c_out = conv_weight.shape[2]
    group = slots * FIELDS
    tables = [jnp.asarray(table, jnp.bfloat16) for table in pick_tables()]
    return pl.pallas_call(
        layer_kernel,
        out_shape=(
            jax.ShapeDtypeStruct((c_in, TAPS * c_out), jnp.bfloat16),
            jax.ShapeDtypeStruct((8, 8 * c_out), jnp.float32),
        ),
        scratch_shapes=[
            pltpu.VMEM((slots * CELLS_UP, c_in), jnp.bfloat16),
            pltpu.VMEM((8 * c_in, 8 * c_out), jnp.bfloat16),
            pltpu.VMEM((8, c_in, slots * COARSE), jnp.bfloat16),
            pltpu.VMEM((slots * COARSE, 8 * c_out), jnp.bfloat16),
            pltpu.VMEM((COARSE, 8 * group), jnp.bfloat16),
            pltpu.VMEM((12 * group, 4 * c_out), jnp.bfloat16),
            pltpu.VMEM((4 * group, 8 * c_out), jnp.float32),
            pltpu.VMEM((1, 8 * c_out), jnp.float32),
        ],
        compiler_params=pltpu.CompilerParams(vmem_limit_bytes=48 * 1024 * 1024),
        cost_estimate=pl.CostEstimate(
            flops=8 * slots * COARSE * TAPS * c_in * c_out,
            bytes_accessed=6 * 1024 * 1024,
            transcendentals=slots * FINE * c_out,
        ),
    )(
        patches,
        work_cot.reshape(group, FINE),
        conv_weight.transpose(1, 0, 2),
        jnp.tile(conv_bias[None, :], (1, 8)),
        jnp.tile(head_weight.T, (1, 4)),
        *tables,
    )


def on_device(patches, destination, cotangent, conv_weight, conv_bias, head_weight):
    owners = lax.axis_size("domain")
    own_rows = patches.shape[0]
    train_rows = cotangent.shape[0]
    c_in, _, c_out = conv_weight.shape
    per_pair = (train_rows + owners - 1) // owners
    slot_total = owners * per_pair
    exchange = functools.partial(
        lax.all_to_all, axis_name="domain", split_axis=0, concat_axis=0, tiled=True
    )

    trainer_ids = jnp.arange(owners, dtype=jnp.int32)
    hits = (destination[:, None] == trainer_ids[None, :]).astype(jnp.int32)
    incoming = exchange(jnp.sum(hits, axis=0))
    earlier = jnp.arange(own_rows)[:, None] > jnp.arange(own_rows)[None, :]
    local_rank = jnp.sum(
        (earlier & (destination[:, None] == destination[None, :])).astype(jnp.int32), axis=1
    )
    before = trainer_ids[:, None] > trainer_ids[None, :]
    starts_in = jnp.sum(jnp.where(before, incoming[None, :], 0), axis=1)
    slot_rank = jnp.arange(per_pair, dtype=jnp.int32)
    slot_place = (starts_in[:, None] + slot_rank[None, :]).reshape(slot_total)
    outgoing = cotangent[jnp.minimum(slot_place, train_rows - 1)]
    arrived = exchange(outgoing.reshape(owners, per_pair, FIELDS, FINE))
    arrived = arrived.reshape(slot_total, FIELDS, FINE)
    work_cot = arrived[destination * per_pair + local_rank]

    part, small = layer(patches, work_cot, conv_weight, conv_bias, head_weight)

    scale = float((owners * own_rows * COARSE) ** (-0.5))
    small = jnp.sum(small.reshape(8, 8, c_out), axis=1)
    small = exchange(jnp.broadcast_to(small[None], (owners, 8, c_out)))
    small = jnp.sum(small, axis=0) * scale
    rows = c_in // owners
    terms = exchange(part.reshape(owners, rows, TAPS * c_out))
    conv = jnp.sum(terms.astype(jnp.float32), axis=0) * scale
    return conv.reshape(rows, TAPS, c_out), small[0], small[4:8].T


def solution(mesh):
    placed = (
        P(("groups", "domain"), None, None),
        P(("groups", "domain")),
        P(("groups", "domain"), None, None),
        P(),
        P(),
        P(),
    )
    return jax.shard_map(
        on_device,
        mesh=mesh,
        in_specs=placed,
        out_specs=(P(("groups", "domain"), None, None), P("groups"), P("groups", None)),
        check_vma=False,
    )
```

time: 238 us -> 84.1 us (0.35)
  the two profiles are of different devices: /device:TPU:0 before, /device:TPU:13 now
where the time goes in v1:
time: 84.1 us; the launch traced here: 83.3 us
  waiting for transfers between devices  24.8 us (29%)
  starting transfers between devices  18.6 us (22%)
  Pallas kernels  13.9 us (17%)
  local copies, waits for them, and re-layouts  13.2 us (16%)
  blocking collectives  9.5 us (11%)
  other arithmetic  2.42 us (3%)
    all_to_all x1, waiting for transfers between devices, on_device(): terms = exchange(part.reshape(owners, rows, TAPS * c_out))  19.6 us
    pallas_call x1, Pallas kernels, layer(): pl.pallas_call(layer_kernel, out_shape=(jax.ShapeDtypeStruct((c_in, TAPS...  13.9 us
    all_to_all x1, blocking collectives, on_device(): small = exchange(jnp.broadcast_to(small[None], (owners, 8, c_out)))  9.5 us
    unnamed x21, local copies, waits for them, and re-layouts  8.52 us
    all_to_all x1, starting transfers between devices, on_device(): incoming = exchange(jnp.sum(hits, axis=0))  6.55 us
    all_to_all x1, starting transfers between devices, on_device(): terms = exchange(part.reshape(owners, rows, TAPS * c_out))  6.04 us
    all_to_all x1, starting transfers between devices, on_device(): arrived = exchange(outgoing.reshape(owners, per_pair, FIELDS, FINE))  6.03 us
    all_to_all x1, waiting for transfers between devices, on_device(): arrived = exchange(outgoing.reshape(owners, per_pair, FIELDS, FINE))  5.17 us
  transfers between devices with their start and end apart: 3, of which 2 were waited for; matrix products, arithmetic and copies ran while one was open for 7% of the time, Pallas kernels for 0%

profile of v1, /device:TPU:13, one launch (start us, length us, event | category | flops | bytes accessed | tf_op | source)
XLA Modules:
  0.0 83.3 jit_solution(6100843476935801945)
XLA Ops:
  0.6 0.9 %convert_reduce_fusion.1 = (s32[16]{0:T(128)S(1)}, s32[16]{0:T(128)S(1)}) fusion(s32[16]{0:T(128)} %param.10), kind=kLoop, calls=%fused_computation.4 | loop fusion | flops 2016 | bytes 192 | tf_op jit(solution)/shard_map/reduce_sum | solution.py:196
  1.6 0.7 copy.25
  2.3 6.6 %all-to-all-start = ((s32[16,1,1]{2,1,0:T(1,128)}), s32[16,1,1]{2,1,0:T(1,128)S(1)}, u32[]{:S(2)}, u32[]{:S(2)}) async-start(s32[16,1,1]{2,1,0:T(1,128)} %copy.25), calls=%async_computation | async-start | bytes 16384 | tf_op jit(solution)/shard_map/all_to_all | solution.py:194
  8.8 1.9 %copy.26 = bf16[256,27,64]{2,0,1:T(8,128)(2,1)S(1)} copy(bf16[256,27,64]{0,2,1:T(8,128)(2,1)} %param.12) | data formatting | bytes 1769472 | tf_op args[3]
  10.7 1.6 %copy.27.patch_ref = bf16[16,125,256]{2,1,0:T(8,128)(2,1)S(1)} copy(bf16[16,125,256]{2,0,1:T(8,128)(2,1)} %param.9) | data formatting | bytes 2048000 | tf_op args[0]
  12.3 0.1 tile.20.head_ref
  12.4 0.1 tile.18.bias_ref
  12.5 0.4 reduce
  12.9 0.1 select_reduce_fusion
  13.1 0.1 min.18
  13.2 1.3 %gather_fusion = bf16[32,4,512]{2,1,0:T(4,128)(2,1)} fusion(bf16[32,4,512]{2,1,0:T(4,128)(2,1)S(1)} %copy-done, s32[1024]{0:T(1024)S(1)} %pad_clamp_fusion.1), kind=kCustom, calls=%fused_computation | custom fusion | bytes 262272 | tf_op jit(solution)/shard_map/gather | solution.py:203
  14.6 6.0 %all-to-all-start.1 = ((bf16[16,2,4,512]{3,2,1,0:T(4,128)(2,1)}), bf16[16,2,4,512]{3,2,1,0:T(4,128)(2,1)S(1)}, u32[]{:S(2)}, u32[]{:S(2)}) async-start(bf16[16,2,4,512]{3,2,1,0:T(4,128)(2,1)} %bitcast.2), calls=%async_computation.1 | async-start | bytes 262144 | tf_op jit(solution)/shard_map/all_to_all | solution.py:204
  20.6 5.2 %all-to-all-done.1 = bf16[16,2,4,512]{3,2,1,0:T(4,128)(2,1)S(1)} async-done(((bf16[16,2,4,512]{3,2,1,0:T(4,128)(2,1)}), bf16[16,2,4,512]{3,2,1,0:T(4,128)(2,1)S(1)}, u32[]{:S(2)}, u32[]{:S(2)}) %all-to-all-start.1) | async-done | bytes 131104 | tf_op jit(solution)/shard_map/all_to_all | solution.py:204
  25.8 0.6 gather_fusion.1
  26.4 1.0 %copy-done.2 = bf16[1024,256]{1,0:T(8,128)(2,1)S(1)} copy-done((bf16[1024,256]{1,0:T(8,128)(2,1)S(1)}, bf16[1024,256]{1,0:T(8,128)(2,1)}, u32[]{:S(2)}) %copy-start.2) | copy-done | bytes 524312
  27.5 1.0 %copy-done.3 = bf16[256,1024]{1,0:T(8,128)(2,1)S(1)} copy-done((bf16[256,1024]{1,0:T(8,128)(2,1)S(1)}, bf16[256,1024]{1,0:T(8,128)(2,1)}, u32[]{:S(2)}) %copy-start.3) | copy-done | bytes 524312
  28.5 1.0 %copy-done.4 = bf16[512,512]{1,0:T(8,128)(2,1)S(1)} copy-done((bf16[512,512]{1,0:T(8,128)(2,1)S(1)}, bf16[512,512]{1,0:T(8,128)(2,1)}, u32[]{:S(2)}) %copy-start.4) | copy-done | bytes 524312
  29.6 13.9 %shard_map.112 = (bf16[256,1728]{1,0:T(8,128)(2,1)S(1)}, f32[8,512]{1,0:T(8,128)S(1)}) custom-call(bf16[16,125,256]{2,1,0:T(8,128)(2,1)S(1)} %copy.27.patch_ref, bf16[64,512]{1,0:T(8,128)(2,1)S(1)} %reshape.80.cot_ref, bf16[27,256,64]{2,1,0:T(8,128)(2,1)S(1)} %bitcast.12, f32[1,512]{1,0:T(1,128)S(1)} %tile.18.bias_ref, f32[4,256]{1,0:T(4,128)S(1)} %tile.20.head_ref, ...), custom_call_target="tpu_custom_call" | custom-call | flops 3623878656 | bytes 6291456 | tf_op jit(solution)/shard_map/pallas_call | solution.py:149
  43.5 0.9 %copy-done.1 = bf16[256,1728]{1,0:T(8,128)(2,1)} copy-done((bf16[256,1728]{1,0:T(8,128)(2,1)}, bf16[256,1728]{1,0:T(8,128)(2,1)S(1)}, u32[]{:S(2)}) %copy-start.1) | copy-done | bytes 884760
  44.4 0.1 reshape.82
  44.5 0.1 reshape.101
  44.6 9.5 %all_to_all.24 = f32[16,1,512]{2,1,0:T(1,128)S(1)} all-to-all(f32[16,1,512]{2,1,0:T(1,128)S(1)} %reshape.101), channel_id=1, replica_groups=mesh['groups'=2,'domain'=16] {'domain'}, dimensions={0} | all-to-all | bytes 65536 | tf_op jit(solution)/shard_map/all_to_all | solution.py:212
  54.1 6.0 %all-to-all-start.2 = ((bf16[16,16,1728]{2,1,0:T(8,128)(2,1)}), bf16[16,16,1728]{2,1,0:T(8,128)(2,1)S(1)}, u32[]{:S(2)}, u32[]{:S(2)}) async-start(bf16[16,16,1728]{2,1,0:T(8,128)(2,1)} %bitcast.13), calls=%async_computation.2 | async-start | bytes 1835008 | tf_op jit(solution)/shard_map/all_to_all | solution.py:215
  60.2 0.5 broadcast.63
  60.7 0.7 reduce.1
  61.4 0.1 reshape.102
  61.5 0.5 slice_bitcast_fusion.1
  62.0 0.6 slice_bitcast_fusion
  62.6 19.6 %all-to-all-done.2 = bf16[16,16,1728]{2,1,0:T(8,128)(2,1)S(1)} async-done(((bf16[16,16,1728]{2,1,0:T(8,128)(2,1)}), bf16[16,16,1728]{2,1,0:T(8,128)(2,1)S(1)}, u32[]{:S(2)}, u32[]{:S(2)}) %all-to-all-start.2) | async-done | bytes 884768 | tf_op jit(solution)/shard_map/all_to_all | solution.py:215
  82.2 0.1 convert_reduce_fusion
  82.4 0.1 mul.22
  82.5 0.8 copy.28
  (26 shorter events, 0.3 us)
Async XLA Ops:
  0.6 12.6 %copy-start = (bf16[32,4,512]{2,1,0:T(4,128)(2,1)S(1)}, bf16[32,4,512]{2,1,0:T(4,128)(2,1)}, u32[]{:S(2)}) copy-start(bf16[32,4,512]{2,1,0:T(4,128)(2,1)} %param.11) | copy-start | bytes 393220
  2.3 10.3 %all-to-all-start = ((s32[16,1,1]{2,1,0:T(1,128)}), s32[16,1,1]{2,1,0:T(1,128)S(1)}, u32[]{:S(2)}, u32[]{:S(2)}) async-start(s32[16,1,1]{2,1,0:T(1,128)} %copy.25), calls=%async_computation | async-start | bytes 16384 | tf_op jit(solution)/shard_map/all_to_all | solution.py:194
  8.8 3.5 %copy-start.5 = (f32[64,4]{0,1:T(4,128)S(1)}, f32[64,4]{0,1:T(4,128)}, u32[]{:S(2)}) copy-start(f32[64,4]{0,1:T(4,128)} %param.14) | copy-start | bytes 3076
  8.8 3.6 %copy-start.7 = (f32[64]{0:T(128)S(1)}, f32[64]{0:T(128)}, u32[]{:S(2)}) copy-start(f32[64]{0:T(128)} %param.13) | copy-start | bytes 772
  10.7 9.9 %copy-start.6 = (s32[16]{0:T(128)S(1)}, s32[16]{0:T(128)}, u32[]{:S(2)}) copy-start(s32[16]{0:T(128)} %param.10) | copy-start | bytes 196
  14.6 11.2 %all-to-all-start.1 = ((bf16[16,2,4,512]{3,2,1,0:T(4,128)(2,1)}), bf16[16,2,4,512]{3,2,1,0:T(4,128)(2,1)S(1)}, u32[]{:S(2)}, u32[]{:S(2)}) async-start(bf16[16,2,4,512]{3,2,1,0:T(4,128)(2,1)} %bitcast.2), calls=%async_computation.1 | async-start | bytes 262144 | tf_op jit(solution)/shard_map/all_to_all | solution.py:204
  26.4 1.0 %copy-start.2 = (bf16[1024,256]{1,0:T(8,128)(2,1)S(1)}, bf16[1024,256]{1,0:T(8,128)(2,1)}, u32[]{:S(2)}) copy-start(bf16[1024,256]{1,0:T(8,128)(2,1)} %constant.5.clone.pick_ref) | copy-start | bytes 1572868
  27.5 1.0 %copy-start.3 = (bf16[256,1024]{1,0:T(8,128)(2,1)S(1)}, bf16[256,1024]{1,0:T(8,128)(2,1)}, u32[]{:S(2)}) copy-start(bf16[256,1024]{1,0:T(8,128)(2,1)} %constant.6.clone.pick_t_ref) | copy-start | bytes 1572868
  28.5 1.0 %copy-start.4 = (bf16[512,512]{1,0:T(8,128)(2,1)S(1)}, bf16[512,512]{1,0:T(8,128)(2,1)}, u32[]{:S(2)}) copy-start(bf16[512,512]{1,0:T(8,128)(2,1)} %constant.7.clone.fine_ref) | copy-start | bytes 1572868
  43.5 0.9 %copy-start.1 = (bf16[256,1728]{1,0:T(8,128)(2,1)}, bf16[256,1728]{1,0:T(8,128)(2,1)S(1)}, u32[]{:S(2)}) copy-start(bf16[256,1728]{1,0:T(8,128)(2,1)S(1)} %get-tuple-element.5) | copy-start | bytes 2654212
  54.1 28.1 %all-to-all-start.2 = ((bf16[16,16,1728]{2,1,0:T(8,128)(2,1)}), bf16[16,16,1728]{2,1,0:T(8,128)(2,1)S(1)}, u32[]{:S(2)}, u32[]{:S(2)}) async-start(bf16[16,16,1728]{2,1,0:T(8,128)(2,1)} %bitcast.13), calls=%async_computation.2 | async-start | bytes 1835008 | tf_op jit(solution)/shard_map/all_to_all | solution.py:215

commit v2 on v1

v2 whole, which is shorter than its diff:
```python
import functools
import itertools

import jax
import jax.numpy as jnp
from jax import lax
from jax.experimental import pallas as pl
from jax.experimental.pallas import tpu as pltpu
from jax.sharding import PartitionSpec as P

FIELDS = 4
TAPS = 27
PS = 4
PAD = 5
CELLS = PAD**3
CELLS_UP = 128
COARSE = PS**3
FINE = 8 * COARSE
BITS = list(itertools.product((0, 1), repeat=3))


def tap_of(shift, parity):
    tap = 0
    for s, q in zip(BITS[shift], BITS[parity]):
        if s == 1 and q == 0:
            return None
        tap = 3 * tap + (1 if q == 0 else (0 if s == 1 else 2))
    return tap


def digits(index):
    return (index >> 4) & 3, (index >> 2) & 3, index & 3


def shifted_cell(index):
    j1, j2, j3 = digits(index & (COARSE - 1))
    shift = index >> 7
    cell = (j1 + (shift >> 2)) * PAD * PAD + (j2 + ((shift >> 1) & 1)) * PAD + j3 + (shift & 1)
    return ((index >> 6) & 1) * CELLS_UP + cell


def fine_cell(index):
    j1, j2, j3 = digits(index & (COARSE - 1))
    parity = index >> 6
    row = 2 * j1 + (parity >> 2)
    return (row * 2 * PS + 2 * j2 + ((parity >> 1) & 1)) * 2 * PS + 2 * j3 + (parity & 1)


def line(shape, axis):
    return lax.broadcasted_iota(jnp.int32, shape, axis)


def one_hot(mask):
    return jnp.where(mask, 1.0, 0.0).astype(jnp.bfloat16)


def dot(a, b, dims=((1,), (0,))):
    return lax.dot_general(a, b, (dims, ((), ())), preferred_element_type=jnp.float32)


def forward_kernel(
    patch_ref, w_ref, bias_ref, hidden_ref, turned_ref, cells, wide, pick, pick_t
):
    slots = patch_ref.shape[0]
    c_in = patch_ref.shape[2]
    c_out = w_ref.shape[2]
    half = 4 * c_out
    bf = jnp.bfloat16
    tall, short = 16 * COARSE, 2 * CELLS_UP

    pick[...] = one_hot(shifted_cell(line((tall, 1), 0)) == line((tall, short), 1))
    pick_t[...] = one_hot(shifted_cell(line((1, tall), 1)) == line((short, tall), 0))
    cells[...] = jnp.zeros_like(cells)
    for p in range(slots):
        cells[p * CELLS_UP : p * CELLS_UP + CELLS, :] = patch_ref[p]
    wide[...] = jnp.zeros_like(wide)
    for s in range(8):
        for q in range(8):
            tap = tap_of(s, q)
            if tap is not None:
                wide[s * c_in : (s + 1) * c_in, q * c_out : (q + 1) * c_out] = w_ref[tap]

    @pl.loop(0, slots // 2)
    def _(pair):
        rows = pl.ds(pl.multiple_of(pair * 2 * COARSE, 2 * COARSE), 2 * COARSE)
        both = cells[pl.ds(pl.multiple_of(pair * short, short), short), :]
        shifted = dot(pick[...], both).astype(bf)
        turn = dot(both, pick_t[...], ((0,), (0,))).astype(bf)
        for s in range(8):
            turned_ref[s, :, rows] = turn[:, s * 2 * COARSE : (s + 1) * 2 * COARSE]
        beside = jnp.concatenate(
            [shifted[s * 2 * COARSE : (s + 1) * 2 * COARSE] for s in range(8)], axis=1
        )
        for h in range(2):
            lanes = slice(h * half, (h + 1) * half)
            deep = (4 + 4 * h) * c_in
            hidden_ref[rows, lanes] = dot(beside[:, :deep], wide[:deep, lanes]) + bias_ref[:, lanes]


def backward_kernel(
    owner_rows, hidden_ref, turned_ref, cot_ref, head_ref, part_ref,
    grads, view, head_big, head_sum, bias_sum,
):
    slots = hidden_ref.shape[0] // COARSE
    half = hidden_ref.shape[1] // 2
    c_out = half // 4
    c_in = part_ref.shape[0]
    group = slots * FIELDS
    quad = 4 * group
    bf = jnp.bfloat16

    fine = one_hot(fine_cell(line((FINE, 1), 0)) == line((FINE, FINE), 1))
    moved = dot(fine, cot_ref[...], ((1,), (1,))).astype(bf)
    for q in range(8):
        view[:, q * group : (q + 1) * group] = moved[q * COARSE : (q + 1) * COARSE]

    row, col = line((quad, half), 0), line((quad, half), 1)
    same = row // group == col // c_out
    spread = jnp.zeros((quad, half), jnp.float32)
    for f in range(FIELDS):
        spread = jnp.where(same & (row % FIELDS == f), head_ref[f : f + 1, :], spread)
    for t in range(3):
        term = spread.astype(bf)
        head_big[t * quad : (t + 1) * quad, :] = term
        spread = spread - term.astype(jnp.float32)

    head_sum[...] = jnp.zeros_like(head_sum)
    bias_sum[...] = jnp.zeros_like(bias_sum)
    lane_slot = line((2 * COARSE, 2 * quad), 1) % group // FIELDS
    row_slot = line((2 * COARSE, 2 * quad), 0) // COARSE

    @pl.loop(0, slots // 2)
    def _(pair):
        rows = pl.ds(pl.multiple_of(pair * 2 * COARSE, 2 * COARSE), 2 * COARSE)
        here = view[...].astype(jnp.float32)
        here = jnp.concatenate([here, here], axis=0)
        here = jnp.where(lane_slot == row_slot + 2 * pair, here, 0.0).astype(bf)
        for h in range(2):
            lanes = slice(h * half, (h + 1) * half)
            hidden = hidden_ref[rows, lanes]
            mine = here[:, h * quad : (h + 1) * quad]
            upstream = dot(jnp.concatenate([mine] * 3, axis=1), head_big[...])
            gate = jax.nn.sigmoid(hidden)
            active = hidden * gate
            grad = upstream * gate * (1.0 + hidden * (1.0 - gate))
            grads[rows, lanes] = grad.astype(bf)
            bias_sum[:, lanes] += jnp.sum(grad, axis=0, keepdims=True)
            top = active.astype(bf)
            rest = (active - top.astype(jnp.float32)).astype(bf)
            head_sum[...] += dot(mine, jnp.concatenate([top, rest], axis=1), ((0,), (0,)))

    for s in range(8):
        for h in range(2):
            if s >= 4 and h == 0:
                continue
            block = dot(turned_ref[s], grads[:, h * half : (h + 1) * half]).astype(bf)
            for r in range(4):
                tap = tap_of(s, 4 * h + r)
                if tap is not None:
                    part_ref[:, tap * c_out : (tap + 1) * c_out] = block[:, r * c_out : (r + 1) * c_out]

    row, col = line((quad, 2 * half), 0), line((quad, 2 * half), 1)
    kept = jnp.where(row // group == col % half // c_out, head_sum[...], 0.0)
    sums = [bias_sum[...]]
    for f in range(FIELDS):
        sums.append(jnp.sum(jnp.where(row % FIELDS == f, kept, 0.0), axis=0, keepdims=True))
    sums = [sum(x[:, g * c_out : (g + 1) * c_out] for g in range(8)) for x in sums]
    tops = [x.astype(bf).astype(jnp.float32) for x in sums]
    tail = tops + [x - top for x, top in zip(sums, tops)]
    place = line((c_in, c_out), 0) % owner_rows
    for b in range(-(-len(tail) // owner_rows)):
        fill = jnp.zeros((c_in, c_out), jnp.float32)
        for i, value in enumerate(tail[b * owner_rows : (b + 1) * owner_rows]):
            fill = jnp.where(place == i, value, fill)
        part_ref[:, (TAPS + b) * c_out : (TAPS + b + 1) * c_out] = fill.astype(bf)


LIMIT = pltpu.CompilerParams(vmem_limit_bytes=32 * 1024 * 1024)


def forward(patches, conv_weight, conv_bias):
    slots, _, c_in = patches.shape
    c_out = conv_weight.shape[2]
    return pl.pallas_call(
        forward_kernel,
        out_shape=(
            jax.ShapeDtypeStruct((slots * COARSE, 8 * c_out), jnp.float32),
            jax.ShapeDtypeStruct((8, c_in, slots * COARSE), jnp.bfloat16),
        ),
        scratch_shapes=[
            pltpu.VMEM((slots * CELLS_UP, c_in), jnp.bfloat16),
            pltpu.VMEM((8 * c_in, 8 * c_out), jnp.bfloat16),
            pltpu.VMEM((16 * COARSE, 2 * CELLS_UP), jnp.bfloat16),
            pltpu.VMEM((2 * CELLS_UP, 16 * COARSE), jnp.bfloat16),
        ],
        compiler_params=LIMIT,
        cost_estimate=pl.CostEstimate(
            flops=8 * slots * COARSE * TAPS * c_in * c_out,
            bytes_accessed=10 * 1024 * 1024,
            transcendentals=0,
        ),
    )(patches, conv_weight.transpose(1, 0, 2), jnp.tile(conv_bias[None, :], (1, 8)))


def backward(hidden, turned, work_cot, head_weight, owner_rows):
    slots = work_cot.shape[0]
    c_in = turned.shape[1]
    c_out = head_weight.shape[0]
    group = slots * FIELDS
    blocks = TAPS + -(-2 * (FIELDS + 1) // owner_rows)
    return pl.pallas_call(
        functools.partial(backward_kernel, owner_rows),
        out_shape=jax.ShapeDtypeStruct((c_in, blocks * c_out), jnp.bfloat16),
        scratch_shapes=[
            pltpu.VMEM((slots * COARSE, 8 * c_out), jnp.bfloat16),
            pltpu.VMEM((COARSE, 8 * group), jnp.bfloat16),
            pltpu.VMEM((12 * group, 4 * c_out), jnp.bfloat16),
            pltpu.VMEM((4 * group, 8 * c_out), jnp.float32),
            pltpu.VMEM((1, 8 * c_out), jnp.float32),
        ],
        compiler_params=LIMIT,
        cost_estimate=pl.CostEstimate(
            flops=8 * slots * COARSE * TAPS * c_in * c_out,
            bytes_accessed=8 * 1024 * 1024,
            transcendentals=slots * FINE * c_out,
        ),
    )(hidden, turned, work_cot.reshape(group, FINE), jnp.tile(head_weight.T, (1, 4)))


def on_device(patches, destination, cotangent, conv_weight, conv_bias, head_weight):
    owners = lax.axis_size("domain")
    own_rows = patches.shape[0]
    train_rows = cotangent.shape[0]
    c_in, _, c_out = conv_weight.shape
    per_pair = (train_rows + owners - 1) // owners
    slot_total = owners * per_pair
    exchange = functools.partial(
        lax.all_to_all, axis_name="domain", split_axis=0, concat_axis=0, tiled=True
    )

    trainer_ids = jnp.arange(owners, dtype=jnp.int32)
    hits = (destination[:, None] == trainer_ids[None, :]).astype(jnp.int32)
    incoming = exchange(jnp.sum(hits, axis=0))
    earlier = jnp.arange(own_rows)[:, None] > jnp.arange(own_rows)[None, :]
    local_rank = jnp.sum(
        (earlier & (destination[:, None] == destination[None, :])).astype(jnp.int32), axis=1
    )
    before = trainer_ids[:, None] > trainer_ids[None, :]
    starts_in = jnp.sum(jnp.where(before, incoming[None, :], 0), axis=1)
    slot_rank = jnp.arange(per_pair, dtype=jnp.int32)
    slot_place = (starts_in[:, None] + slot_rank[None, :]).reshape(slot_total)
    outgoing = cotangent[jnp.minimum(slot_place, train_rows - 1)]
    patches, outgoing = lax.optimization_barrier((patches, outgoing))
    arrived = exchange(outgoing.reshape(owners, per_pair, FIELDS, FINE))
    hidden, turned = forward(patches, conv_weight, conv_bias)
    arrived = arrived.reshape(slot_total, FIELDS, FINE)
    work_cot = arrived[destination * per_pair + local_rank]

    rows = c_in // owners
    part = backward(hidden, turned, work_cot, head_weight, rows)
    terms = exchange(part.reshape(owners, rows, -1)).astype(jnp.float32)
    scale = float((owners * own_rows * COARSE) ** (-0.5))
    sums = jnp.sum(terms, axis=0) * scale
    conv = sums[:, : TAPS * c_out].reshape(rows, TAPS, c_out)
    tail = sums[:, TAPS * c_out :].reshape(rows, -1, c_out).transpose(1, 0, 2).reshape(-1, c_out)
    small = tail[: FIELDS + 1] + tail[FIELDS + 1 : 2 * (FIELDS + 1)]
    return conv, small[0], small[1:].T


def solution(mesh):
    placed = (
        P(("groups", "domain"), None, None),
        P(("groups", "domain")),
        P(("groups", "domain"), None, None),
        P(),
        P(),
        P(),
    )
    return jax.shard_map(
        on_device,
        mesh=mesh,
        in_specs=placed,
        out_specs=(P(("groups", "domain"), None, None), P("groups"), P("groups", None)),
        check_vma=False,
    )
```

time: 84.1 us -> 74.4 us (0.88)
  the two profiles are of different devices: /device:TPU:13 before, /device:TPU:1 now
where the time goes in v2:
time: 74.4 us; the launch traced here: 74 us
  blocking collectives  28.7 us (39%)
  local copies, waits for them, and re-layouts  15.5 us (21%)
  Pallas kernels  13.2 us (18%)
  starting transfers between devices  11.7 us (16%)
  other arithmetic  2.41 us (3%)
  waiting for transfers between devices  1.64 us (2%)
  between operations  0.76 us (1%)
    all_to_all x1, blocking collectives, on_device(): terms = exchange(part.reshape(owners, rows, -1)).astype(jnp.float32)  28.7 us
    unnamed x14, local copies, waits for them, and re-layouts  9.74 us
    all_to_all x1, starting transfers between devices, on_device(): incoming = exchange(jnp.sum(hits, axis=0))  7.35 us
    pallas_call x1, Pallas kernels, forward(): pl.pallas_call(forward_kernel, out_shape=(jax.ShapeDtypeStruct((slots * C...  7.08 us
    pallas_call x1, Pallas kernels, backward(): pl.pallas_call(functools.partial(backward_kernel, owner_rows), out_shape=...  6.12 us
    all_to_all x1, starting transfers between devices, on_device(): arrived = exchange(outgoing.reshape(owners, per_pair, FIELDS, FINE))  4.39 us
    all_to_all x1, waiting for transfers between devices, on_device(): incoming = exchange(jnp.sum(hits, axis=0))  1.64 us
  transfers between devices with their start and end apart: 2, of which 1 were waited for; matrix products, arithmetic and copies ran while one was open for 6% of the time, Pallas kernels for 10%

profile of v2, /device:TPU:1, one launch (start us, length us, event | category | flops | bytes accessed | tf_op | source)
XLA Modules:
  0.0 74.0 jit_solution(7976401057501014232)
XLA Ops:
  0.6 0.0 copy-start
  0.7 1.0 %convert_reduce_fusion.1 = (s32[16]{0:T(128)S(1)}, s32[16]{0:T(128)S(1)}) fusion(s32[16]{0:T(128)} %param.7), kind=kLoop, calls=%fused_computation.4 | loop fusion | flops 2016 | bytes 192 | tf_op jit(solution)/shard_map/reduce_sum | solution.py:245
  1.6 0.7 copy.22
  2.3 7.3 %all-to-all-start = ((s32[16,1,1]{2,1,0:T(1,128)}), s32[16,1,1]{2,1,0:T(1,128)S(1)}, u32[]{:S(2)}, u32[]{:S(2)}) async-start(s32[16,1,1]{2,1,0:T(1,128)} %copy.22), calls=%async_computation | async-start | bytes 16384 | tf_op jit(solution)/shard_map/all_to_all | solution.py:243
  9.6 0.7 compare_select_fusion
  10.3 0.7 tile.8
  11.0 0.1 tile.18.bias_ref
  11.1 0.7 tile.19
  11.7 0.1 tile.20.head_ref
  11.8 1.9 %copy.23 = bf16[256,27,64]{2,0,1:T(8,128)(2,1)S(1)} copy(bf16[256,27,64]{0,2,1:T(8,128)(2,1)} %param.9) | data formatting | bytes 1769472 | tf_op args[3]
  13.7 1.6 %all-to-all-done = s32[16,1,1]{2,1,0:T(1,128)S(1)} async-done(((s32[16,1,1]{2,1,0:T(1,128)}), s32[16,1,1]{2,1,0:T(1,128)S(1)}, u32[]{:S(2)}, u32[]{:S(2)}) %all-to-all-start) | async-done | bytes 96 | tf_op jit(solution)/shard_map/all_to_all | solution.py:243
  15.4 0.4 reduce
  15.7 0.1 select_reduce_fusion
  15.9 0.1 add_minimum_fusion
  15.9 0.1 min.18
  16.1 1.3 %gather_fusion = bf16[32,4,512]{2,1,0:T(4,128)(2,1)} fusion(bf16[32,4,512]{2,1,0:T(4,128)(2,1)S(1)} %copy-done, s32[1024]{0:T(1024)S(1)} %pad_clamp_fusion.1), kind=kCustom, calls=%fused_computation | custom fusion | bytes 262272 | tf_op jit(solution)/shard_map/gather | solution.py:252
  17.4 4.4 %all-to-all-start.1 = ((bf16[16,2,4,512]{3,2,1,0:T(4,128)(2,1)}), bf16[16,2,4,512]{3,2,1,0:T(4,128)(2,1)S(1)}, u32[]{:S(2)}, u32[]{:S(2)}) async-start(bf16[16,2,4,512]{3,2,1,0:T(4,128)(2,1)} %bitcast.3), calls=%async_computation.1 | async-start | bytes 262144 | tf_op jit(solution)/shard_map/all_to_all | solution.py:254
  21.8 0.3 copy.24.patch_ref
  22.1 7.1 %shard_map.85 = (f32[1024,512]{1,0:T(8,128)S(1)}, bf16[8,256,1024]{2,1,0:T(8,128)(2,1)S(1)}) custom-call(bf16[16,125,256]{2,1,0:T(8,128)(2,1)S(1)} %copy.24.patch_ref, bf16[27,256,64]{2,1,0:T(8,128)(2,1)S(1)} %bitcast.13, f32[1,512]{1,0:T(1,128)S(1)} %tile.18.bias_ref), custom_call_target="tpu_custom_call" | custom-call | flops 3623878656 | bytes 10485760 | tf_op jit(solution)/shard_map/pallas_call | solution.py:184
  29.2 1.9 %copy-done.1 = bf16[8,256,1024]{2,1,0:T(8,128)(2,1)} copy-done((bf16[8,256,1024]{2,1,0:T(8,128)(2,1)}, bf16[8,256,1024]{2,1,0:T(8,128)(2,1)S(1)}, u32[]{:S(2)}) %copy-start.1) | copy-done | bytes 4194328
  31.1 1.3 %copy-done.3 = f32[1024,512]{1,0:T(8,128)} copy-done((f32[1024,512]{1,0:T(8,128)}, f32[1024,512]{1,0:T(8,128)S(1)}, u32[]{:S(2)}) %copy-start.3) | copy-done | bytes 2097176
  32.5 0.6 gather_fusion.1
  33.1 2.2 %copy-done.2 = bf16[8,256,1024]{2,1,0:T(8,128)(2,1)S(1)} copy-done((bf16[8,256,1024]{2,1,0:T(8,128)(2,1)S(1)}, bf16[8,256,1024]{2,1,0:T(8,128)(2,1)}, u32[]{:S(2)}) %copy-start.2) | copy-done | bytes 4194328
  35.3 1.6 %copy-done.4 = f32[1024,512]{1,0:T(8,128)S(1)} copy-done((f32[1024,512]{1,0:T(8,128)S(1)}, f32[1024,512]{1,0:T(8,128)}, u32[]{:S(2)}) %copy-start.4) | copy-done | bytes 2097176
  36.9 6.1 %shard_map.86 = bf16[256,1792]{1,0:T(8,128)(2,1)S(1)} custom-call(f32[1024,512]{1,0:T(8,128)S(1)} %copy-done.4, bf16[8,256,1024]{2,1,0:T(8,128)(2,1)S(1)} %copy-done.2, bf16[64,512]{1,0:T(8,128)(2,1)S(1)} %reshape.75.cot_ref, f32[4,256]{1,0:T(4,128)S(1)} %tile.20.head_ref), custom_call_target="tpu_custom_call" | custom-call | flops 3623878656 | bytes 8388608 | tf_op jit(solution)/shard_map/pallas_call | solution.py:211
  43.0 28.7 %all_to_all.19 = bf16[16,16,1792]{2,1,0:T(8,128)(2,1)S(1)} all-to-all(bf16[16,16,1792]{2,1,0:T(8,128)(2,1)S(1)} %bitcast.14), channel_id=1, replica_groups=mesh['groups'=2,'domain'=16] {'domain'}, dimensions={0} | all-to-all | bytes 1835008 | tf_op jit(solution)/shard_map/all_to_all | solution.py:261
  71.8 0.1 convert_reduce_fusion
  71.9 0.1 slice_add_fusion
  72.0 0.5 slice_bitcast_fusion.1
  72.5 0.6 slice_bitcast_fusion
  73.1 0.1 reshape.77
  73.2 0.8 %copy.25 = f32[16,27,64]{2,0,1:T(8,128)} copy(f32[16,27,64]{2,1,0:T(8,128)S(1)} %reshape.77) | data formatting | bytes 221184
  (13 shorter events, 0.1 us)
Async XLA Ops:
  0.6 15.4 %copy-start = (bf16[32,4,512]{2,1,0:T(4,128)(2,1)S(1)}, bf16[32,4,512]{2,1,0:T(4,128)(2,1)}, u32[]{:S(2)}) copy-start(bf16[32,4,512]{2,1,0:T(4,128)(2,1)} %param.8) | copy-start | bytes 393220
  0.6 21.1 %copy-start.5 = (bf16[16,125,256]{2,0,1:T(8,128)(2,1)S(1)}, bf16[16,125,256]{2,0,1:T(8,128)(2,1)}, u32[]{:S(2)}) copy-start(bf16[16,125,256]{2,0,1:T(8,128)(2,1)} %param.6) | copy-start | bytes 3072004
  2.3 13.1 %all-to-all-start = ((s32[16,1,1]{2,1,0:T(1,128)}), s32[16,1,1]{2,1,0:T(1,128)S(1)}, u32[]{:S(2)}, u32[]{:S(2)}) async-start(s32[16,1,1]{2,1,0:T(1,128)} %copy.22), calls=%async_computation | async-start | bytes 16384 | tf_op jit(solution)/shard_map/all_to_all | solution.py:243
  17.4 15.1 %all-to-all-start.1 = ((bf16[16,2,4,512]{3,2,1,0:T(4,128)(2,1)}), bf16[16,2,4,512]{3,2,1,0:T(4,128)(2,1)S(1)}, u32[]{:S(2)}, u32[]{:S(2)}) async-start(bf16[16,2,4,512]{3,2,1,0:T(4,128)(2,1)} %bitcast.3), calls=%async_computation.1 | async-start | bytes 262144 | tf_op jit(solution)/shard_map/all_to_all | solution.py:254
  29.2 1.9 %copy-start.1 = (bf16[8,256,1024]{2,1,0:T(8,128)(2,1)}, bf16[8,256,1024]{2,1,0:T(8,128)(2,1)S(1)}, u32[]{:S(2)}) copy-start(bf16[8,256,1024]{2,1,0:T(8,128)(2,1)S(1)} %get-tuple-element.9.turned_ref) | copy-start | bytes 12582916
  31.1 1.3 %copy-start.3 = (f32[1024,512]{1,0:T(8,128)}, f32[1024,512]{1,0:T(8,128)S(1)}, u32[]{:S(2)}) copy-start(f32[1024,512]{1,0:T(8,128)S(1)} %get-tuple-element.8.hidden_ref) | copy-start | bytes 6291460
  33.1 2.2 %copy-start.2 = (bf16[8,256,1024]{2,1,0:T(8,128)(2,1)S(1)}, bf16[8,256,1024]{2,1,0:T(8,128)(2,1)}, u32[]{:S(2)}) copy-start(bf16[8,256,1024]{2,1,0:T(8,128)(2,1)} %copy-done.1) | copy-start | bytes 12582916
  35.3 1.6 %copy-start.4 = (f32[1024,512]{1,0:T(8,128)S(1)}, f32[1024,512]{1,0:T(8,128)}, u32[]{:S(2)}) copy-start(f32[1024,512]{1,0:T(8,128)} %copy-done.3) | copy-start | bytes 6291460

commit v3 on v2

--- a/solution.py
+++ b/solution.py
@@ -153,7 +153,7 @@
         for h in range(2):
             if s >= 4 and h == 0:
                 continue
-            block = dot(turned_ref[s], grads[:, h * half : (h + 1) * half]).astype(bf)
+            block = dot(turned_ref[s], grads[:, h * half : (h + 1) * half])
             for r in range(4):
                 tap = tap_of(s, 4 * h + r)
                 if tap is not None:
@@ -164,18 +164,124 @@
     sums = [bias_sum[...]]
     for f in range(FIELDS):
         sums.append(jnp.sum(jnp.where(row % FIELDS == f, kept, 0.0), axis=0, keepdims=True))
-    sums = [sum(x[:, g * c_out : (g + 1) * c_out] for g in range(8)) for x in sums]
-    tops = [x.astype(bf).astype(jnp.float32) for x in sums]
-    tail = tops + [x - top for x, top in zip(sums, tops)]
+    tail = 2 * [sum(x[:, g * c_out : (g + 1) * c_out] for g in range(8)) for x in sums]
     place = line((c_in, c_out), 0) % owner_rows
     for b in range(-(-len(tail) // owner_rows)):
         fill = jnp.zeros((c_in, c_out), jnp.float32)
         for i, value in enumerate(tail[b * owner_rows : (b + 1) * owner_rows]):
             fill = jnp.where(place == i, value, fill)
-        part_ref[:, (TAPS + b) * c_out : (TAPS + b + 1) * c_out] = fill.astype(bf)
-
-
-LIMIT = pltpu.CompilerParams(vmem_limit_bytes=32 * 1024 * 1024)
+        part_ref[:, (TAPS + b) * c_out : (TAPS + b + 1) * c_out] = fill
+
+
+def reduce_kernel(
+    c_out, scale, part_ref, out_ref, got, outgoing, landed, send_pair, recv_pair, send_far, recv_far
+):
+    peers, _, rows, width = part_ref.shape
+    me = lax.axis_index("domain")
+    side = lax.rem(me, 2)
+    home = me // 2
+    partner = me + 1 - 2 * side
+    edge = TAPS * c_out
+
+    barrier = pltpu.get_barrier_semaphore()
+    pl.semaphore_signal(
+        barrier, inc=1, device_id={"domain": partner}, device_id_type=pl.DeviceIdType.MESH
+    )
+
+    @pl.loop(1, peers)
+    def _(step):
+        pl.semaphore_signal(
+            barrier,
+            inc=1,
+            device_id={"domain": 2 * lax.rem(home + step, peers) + side},
+            device_id_type=pl.DeviceIdType.MESH,
+        )
+
+    pl.semaphore_wait(barrier, peers)
+
+    def near(block):
+        return pltpu.make_async_remote_copy(
+            src_ref=part_ref.at[block, 1 - side],
+            dst_ref=got.at[block],
+            send_sem=send_pair.at[block],
+            recv_sem=recv_pair.at[block],
+            device_id={"domain": partner},
+            device_id_type=pl.DeviceIdType.MESH,
+        )
+
+    def far(block, slot):
+        return pltpu.make_async_remote_copy(
+            src_ref=outgoing.at[block],
+            dst_ref=landed.at[slot],
+            send_sem=send_far.at[block],
+            recv_sem=recv_far.at[slot],
+            device_id={"domain": 2 * block + side},
+            device_id_type=pl.DeviceIdType.MESH,
+        )
+
+    @pl.loop(1, peers + 1)
+    def _(step):
+        near(lax.rem(home + step, peers)).start()
+
+    spot = line((rows, width), 0) + (line((rows, width), 1) - edge) // c_out * rows
+    in_tail = line((rows, width), 1) >= edge
+    low = in_tail & (spot >= FIELDS + 1)
+
+    def pair_sum(block):
+        near(block).wait_recv()
+        both = part_ref[block, side] + got[block]
+        top = both.astype(jnp.bfloat16).astype(jnp.float32)
+        return jnp.where(low, both - top, jnp.where(in_tail, top, both))
+
+    @pl.loop(1, peers)
+    def _(step):
+        block = lax.rem(home + step, peers)
+        outgoing[block] = pair_sum(block).astype(jnp.bfloat16)
+        far(block, home).start()
+
+    out_ref[...] = pair_sum(home)
+
+    @pl.loop(1, peers)
+    def _(step):
+        source = lax.rem(home + peers - step, peers)
+        far(source, source).wait_recv()
+        out_ref[...] += landed[source].astype(jnp.float32)
+
+    out_ref[...] *= scale
+
+    @pl.loop(1, peers)
+    def _(step):
+        block = lax.rem(home + step, peers)
+        near(block).wait_send()
+        far(block, home).wait_send()
+
+    near(home).wait_send()
+
+
+LIMIT = pltpu.CompilerParams(vmem_limit_bytes=22 * 1024 * 1024)
+
+
+def add_up(part, c_out, owners, scale):
+    rows, width = part.shape[0] // owners, part.shape[1]
+    peers = owners // 2
+    return pl.pallas_call(
+        functools.partial(reduce_kernel, c_out, scale),
+        out_shape=jax.ShapeDtypeStruct((rows, width), jnp.float32),
+        in_specs=[pl.BlockSpec(memory_space=pltpu.VMEM)],
+        out_specs=pl.BlockSpec(memory_space=pltpu.VMEM),
+        scratch_shapes=[
+            pltpu.VMEM((peers, rows, width), jnp.float32),
+            pltpu.VMEM((peers, rows, width), jnp.bfloat16),
+            pltpu.VMEM((peers, rows, width), jnp.bfloat16),
+            pltpu.SemaphoreType.DMA((peers,)),
+            pltpu.SemaphoreType.DMA((peers,)),
+            pltpu.SemaphoreType.DMA((peers,)),
+            pltpu.SemaphoreType.DMA((peers,)),
+        ],
+        compiler_params=pltpu.CompilerParams(
+            collective_id=0, has_side_effects=True, vmem_limit_bytes=22 * 1024 * 1024
+        ),
+    )(part.reshape(peers, 2, rows, width))
 
 
 def forward(patches, conv_weight, conv_bias):
@@ -210,7 +316,7 @@
     blocks = TAPS + -(-2 * (FIELDS + 1) // owner_rows)
     return pl.pallas_call(
         functools.partial(backward_kernel, owner_rows),
-        out_shape=jax.ShapeDtypeStruct((c_in, blocks * c_out), jnp.bfloat16),
+        out_shape=jax.ShapeDtypeStruct((c_in, blocks * c_out), jnp.float32),
         scratch_shapes=[
             pltpu.VMEM((slots * COARSE, 8 * c_out), jnp.bfloat16),
             pltpu.VMEM((COARSE, 8 * group), jnp.bfloat16),
@@ -258,9 +364,8 @@
 
     rows = c_in // owners
     part = backward(hidden, turned, work_cot, head_weight, rows)
-    terms = exchange(part.reshape(owners, rows, -1)).astype(jnp.float32)
     scale = float((owners * own_rows * COARSE) ** (-0.5))
-    sums = jnp.sum(terms, axis=0) * scale
+    sums = add_up(part, c_out, owners, scale)
     conv = sums[:, : TAPS * c_out].reshape(rows, TAPS, c_out)
     tail = sums[:, TAPS * c_out :].reshape(rows, -1, c_out).transpose(1, 0, 2).reshape(-1, c_out)
     small = tail[: FIELDS + 1] + tail[FIELDS + 1 : 2 * (FIELDS + 1)]

time: 74.4 us -> 61.3 us (0.82)
  the two profiles are of different devices: /device:TPU:1 before, /device:TPU:13 now
where the time goes in v3:
time: 61.3 us; the launch traced here: 60.9 us
  Pallas kernels  29.8 us (49%)
  local copies, waits for them, and re-layouts  15.5 us (25%)
  starting transfers between devices  12.6 us (21%)
  other arithmetic  2.27 us (4%)
  between operations  0.76 us (1%)
    pallas_call x1, Pallas kernels, add_up(): pl.pallas_call(functools.partial(reduce_kernel, c_out, scale), out_shape=...  16.5 us
    unnamed x14, local copies, waits for them, and re-layouts  9.75 us
    pallas_call x1, Pallas kernels, forward(): pl.pallas_call(forward_kernel, out_shape=(jax.ShapeDtypeStruct((slots * C...  7.08 us
    all_to_all x1, starting transfers between devices, on_device(): incoming = exchange(jnp.sum(hits, axis=0))  6.55 us
    pallas_call x1, Pallas kernels, backward(): pl.pallas_call(functools.partial(backward_kernel, owner_rows), out_shape=...  6.13 us
    all_to_all x1, starting transfers between devices, on_device(): arrived = exchange(outgoing.reshape(owners, per_pair, FIELDS, FINE))  6.02 us
    gather x1, local copies, waits for them, and re-layouts, on_device(): outgoing = cotangent[jnp.minimum(slot_place, train_rows - 1)]  1.32 us
  transfers between devices with their start and end apart: 2, of which 0 were waited for; matrix products, arithmetic and copies ran while one was open for 7% of the time, Pallas kernels for 12%

profile of v3, /device:TPU:13, one launch (start us, length us, event | category | flops | bytes accessed | tf_op | source)
XLA Modules:
  0.0 60.9 jit_solution(3906655235378186062)
XLA Ops:
  0.6 0.0 copy-start
  0.7 1.0 %convert_reduce_fusion = (s32[16]{0:T(128)S(1)}, s32[16]{0:T(128)S(1)}) fusion(s32[16]{0:T(128)} %param.7), kind=kLoop, calls=%fused_computation.2 | loop fusion | flops 2016 | bytes 192 | tf_op jit(solution)/shard_map/reduce_sum | solution.py:351
  1.6 0.7 %copy.23 = s32[16,1,1]{2,1,0:T(1,128)} copy(s32[16,1,1]{0,2,1:T(1,128)S(1)} %bitcast.18) | data formatting | bytes 128 | tf_op jit(solution)/shard_map/all_to_all | solution.py:349
  2.3 6.6 %all-to-all-start = ((s32[16,1,1]{2,1,0:T(1,128)}), s32[16,1,1]{2,1,0:T(1,128)S(1)}, u32[]{:S(2)}, u32[]{:S(2)}) async-start(s32[16,1,1]{2,1,0:T(1,128)} %copy.23), calls=%async_computation | async-start | bytes 16384 | tf_op jit(solution)/shard_map/all_to_all | solution.py:349
  8.9 0.7 %compare_select_fusion = s32[16]{0:T(128)S(1)} fusion(s32[16]{0:T(128)S(1)} %get-tuple-element.26, s32[16]{0:T(128)} %param.7), kind=kLoop, calls=%fused_computation.12 | loop fusion | flops 80 | bytes 192 | tf_op jit(solution)/shard_map/select_n | solution.py:363
  9.5 0.7 %tile.8 = f32[8,64]{1,0:T(8,128)S(1)} broadcast(f32[64]{0:T(128)} %param.10), dimensions={1} | broadcast | bytes 2304 | tf_op jit(solution)/shard_map/tile | solution.py:308
  10.2 0.1 tile.18.bias_ref
  10.3 0.7 %tile.19 = f32[4,4,64]{2,1,0:T(4,128)S(1)} broadcast(f32[4,64]{1,0:T(4,128)} %bitcast.17), dimensions={0,2} | broadcast | bytes 5120 | tf_op jit(solution)/shard_map/tile | solution.py:333
  10.9 0.1 tile.20.head_ref
  11.0 1.9 %copy.24 = bf16[256,27,64]{2,0,1:T(8,128)(2,1)S(1)} copy(bf16[256,27,64]{0,2,1:T(8,128)(2,1)} %param.9) | data formatting | bytes 1769472 | tf_op args[3]
  12.9 0.0 all-to-all-done
  12.9 0.4 reduce
  13.3 0.1 select_reduce_fusion
  13.4 0.1 add_minimum_fusion
  13.5 0.1 min.18
  13.6 1.3 %gather_fusion = bf16[32,4,512]{2,1,0:T(4,128)(2,1)} fusion(bf16[32,4,512]{2,1,0:T(4,128)(2,1)S(1)} %copy-done, s32[1024]{0:T(1024)S(1)} %pad_clamp_fusion.1), kind=kCustom, calls=%fused_computation | custom fusion | bytes 262272 | tf_op jit(solution)/shard_map/gather | solution.py:358
  15.0 6.0 %all-to-all-start.1 = ((bf16[16,2,4,512]{3,2,1,0:T(4,128)(2,1)}), bf16[16,2,4,512]{3,2,1,0:T(4,128)(2,1)S(1)}, u32[]{:S(2)}, u32[]{:S(2)}) async-start(bf16[16,2,4,512]{3,2,1,0:T(4,128)(2,1)} %bitcast.3), calls=%async_computation.1 | async-start | bytes 262144 | tf_op jit(solution)/shard_map/all_to_all | solution.py:360
  21.0 0.3 copy.25.patch_ref
  21.3 7.1 %shard_map.85 = (f32[1024,512]{1,0:T(8,128)S(1)}, bf16[8,256,1024]{2,1,0:T(8,128)(2,1)S(1)}) custom-call(bf16[16,125,256]{2,1,0:T(8,128)(2,1)S(1)} %copy.25.patch_ref, bf16[27,256,64]{2,1,0:T(8,128)(2,1)S(1)} %bitcast.14, f32[1,512]{1,0:T(1,128)S(1)} %tile.18.bias_ref), custom_call_target="tpu_custom_call" | custom-call | flops 3623878656 | bytes 10485760 | tf_op jit(solution)/shard_map/pallas_call | solution.py:290
  28.4 1.9 %copy-done.1 = bf16[8,256,1024]{2,1,0:T(8,128)(2,1)} copy-done((bf16[8,256,1024]{2,1,0:T(8,128)(2,1)}, bf16[8,256,1024]{2,1,0:T(8,128)(2,1)S(1)}, u32[]{:S(2)}) %copy-start.1) | copy-done | bytes 4194328
  30.4 1.3 %copy-done.3 = f32[1024,512]{1,0:T(8,128)} copy-done((f32[1024,512]{1,0:T(8,128)}, f32[1024,512]{1,0:T(8,128)S(1)}, u32[]{:S(2)}) %copy-start.3) | copy-done | bytes 2097176
  31.7 0.0 all-to-all-done.1
  31.7 0.6 %gather_fusion.1 = bf16[16,4,512]{2,1,0:T(4,128)(2,1)S(1)} fusion(bf16[32,4,512]{2,1,0:T(4,128)(2,1)S(1)} %bitcast.16, s32[1024]{0:T(1024)S(1)} %pad_clamp_fusion), kind=kCustom, calls=%fused_computation.1 | custom fusion | bytes 131136 | tf_op jit(solution)/shard_map/gather | solution.py:363
  32.3 2.2 %copy-done.2 = bf16[8,256,1024]{2,1,0:T(8,128)(2,1)S(1)} copy-done((bf16[8,256,1024]{2,1,0:T(8,128)(2,1)S(1)}, bf16[8,256,1024]{2,1,0:T(8,128)(2,1)}, u32[]{:S(2)}) %copy-start.2) | copy-done | bytes 4194328
  34.5 1.6 %copy-done.4 = f32[1024,512]{1,0:T(8,128)S(1)} copy-done((f32[1024,512]{1,0:T(8,128)S(1)}, f32[1024,512]{1,0:T(8,128)}, u32[]{:S(2)}) %copy-start.4) | copy-done | bytes 2097176
  36.1 6.1 %shard_map.86 = f32[256,1792]{1,0:T(8,128)S(1)} custom-call(f32[1024,512]{1,0:T(8,128)S(1)} %copy-done.4, bf16[8,256,1024]{2,1,0:T(8,128)(2,1)S(1)} %copy-done.2, bf16[64,512]{1,0:T(8,128)(2,1)S(1)} %reshape.75.cot_ref, f32[4,256]{1,0:T(4,128)S(1)} %tile.20.head_ref), custom_call_target="tpu_custom_call" | custom-call | flops 3623878656 | bytes 8388608 | tf_op jit(solution)/shard_map/pallas_call | solution.py:317
  42.2 16.5 %shard_map.87 = f32[16,1792]{1,0:T(8,128)S(1)} custom-call(f32[8,2,16,1792]{3,2,1,0:T(8,128)S(1)} %bitcast.13), custom_call_target="tpu_custom_call" | custom-call | tf_op jit(solution)/shard_map/pallas_call | solution.py:267
  58.8 0.1 slice_add_fusion
  58.9 0.5 slice_bitcast_fusion.1
  59.4 0.6 slice_bitcast_fusion
  60.0 0.1 reshape.77
  60.1 0.8 %copy.26 = f32[16,27,64]{2,0,1:T(8,128)} copy(f32[16,27,64]{2,1,0:T(8,128)S(1)} %reshape.77) | data formatting | bytes 221184
  (11 shorter events, 0.1 us)
Async XLA Ops:
  0.6 13.0 %copy-start = (bf16[32,4,512]{2,1,0:T(4,128)(2,1)S(1)}, bf16[32,4,512]{2,1,0:T(4,128)(2,1)}, u32[]{:S(2)}) copy-start(bf16[32,4,512]{2,1,0:T(4,128)(2,1)} %param.8) | copy-start | bytes 393220
  0.6 20.3 %copy-start.5 = (bf16[16,125,256]{2,0,1:T(8,128)(2,1)S(1)}, bf16[16,125,256]{2,0,1:T(8,128)(2,1)}, u32[]{:S(2)}) copy-start(bf16[16,125,256]{2,0,1:T(8,128)(2,1)} %param.6) | copy-start | bytes 3072004
  2.3 10.6 %all-to-all-start = ((s32[16,1,1]{2,1,0:T(1,128)}), s32[16,1,1]{2,1,0:T(1,128)S(1)}, u32[]{:S(2)}, u32[]{:S(2)}) async-start(s32[16,1,1]{2,1,0:T(1,128)} %copy.23), calls=%async_computation | async-start | bytes 16384 | tf_op jit(solution)/shard_map/all_to_all | solution.py:349
  15.0 16.7 %all-to-all-start.1 = ((bf16[16,2,4,512]{3,2,1,0:T(4,128)(2,1)}), bf16[16,2,4,512]{3,2,1,0:T(4,128)(2,1)S(1)}, u32[]{:S(2)}, u32[]{:S(2)}) async-start(bf16[16,2,4,512]{3,2,1,0:T(4,128)(2,1)} %bitcast.3), calls=%async_computation.1 | async-start | bytes 262144 | tf_op jit(solution)/shard_map/all_to_all | solution.py:360
  28.4 1.9 %copy-start.1 = (bf16[8,256,1024]{2,1,0:T(8,128)(2,1)}, bf16[8,256,1024]{2,1,0:T(8,128)(2,1)S(1)}, u32[]{:S(2)}) copy-start(bf16[8,256,1024]{2,1,0:T(8,128)(2,1)S(1)} %get-tuple-element.9.turned_ref) | copy-start | bytes 12582916
  30.4 1.3 %copy-start.3 = (f32[1024,512]{1,0:T(8,128)}, f32[1024,512]{1,0:T(8,128)S(1)}, u32[]{:S(2)}) copy-start(f32[1024,512]{1,0:T(8,128)S(1)} %get-tuple-element.8.hidden_ref) | copy-start | bytes 6291460
  32.3 2.2 %copy-start.2 = (bf16[8,256,1024]{2,1,0:T(8,128)(2,1)S(1)}, bf16[8,256,1024]{2,1,0:T(8,128)(2,1)}, u32[]{:S(2)}) copy-start(bf16[8,256,1024]{2,1,0:T(8,128)(2,1)} %copy-done.1) | copy-start | bytes 12582916
  34.5 1.6 %copy-start.4 = (f32[1024,512]{1,0:T(8,128)S(1)}, f32[1024,512]{1,0:T(8,128)}, u32[]{:S(2)}) copy-start(f32[1024,512]{1,0:T(8,128)} %copy-done.3) | copy-start | bytes 6291460

commit v4 on v3

--- a/solution.py
+++ b/solution.py
@@ -59,7 +59,8 @@
 
 
 def forward_kernel(
-    patch_ref, w_ref, bias_ref, hidden_ref, turned_ref, cells, wide, pick, pick_t
+    patch_ref, w_ref, bias_ref, hidden_out, turned_out,
+    hidden_ref, turned_ref, cells, wide, pick, pick_t, hidden_sem, turned_sem,
 ):
     slots = patch_ref.shape[0]
     c_in = patch_ref.shape[2]
@@ -80,6 +81,15 @@
             if tap is not None:
                 wide[s * c_in : (s + 1) * c_in, q * c_out : (q + 1) * c_out] = w_ref[tap]
 
+    def leave(pair):
+        rows = pl.ds(pl.multiple_of(pair * 2 * COARSE, 2 * COARSE), 2 * COARSE)
+        return (
+            pltpu.make_async_copy(hidden_ref.at[rows, :], hidden_out.at[rows, :], hidden_sem.at[pair]),
+            pltpu.make_async_copy(
+                turned_ref.at[:, :, rows], turned_out.at[:, :, rows], turned_sem.at[pair]
+            ),
+        )
+
     @pl.loop(0, slots // 2)
     def _(pair):
         rows = pl.ds(pl.multiple_of(pair * 2 * COARSE, 2 * COARSE), 2 * COARSE)
@@ -95,12 +105,31 @@
             lanes = slice(h * half, (h + 1) * half)
             deep = (4 + 4 * h) * c_in
             hidden_ref[rows, lanes] = dot(beside[:, :deep], wide[:deep, lanes]) + bias_ref[:, lanes]
+        for copy in leave(pair):
+            copy.start()
+
+    @pl.loop(0, slots // 2)
+    def _(pair):
+        for copy in leave(pair):
+            copy.wait()
 
 
 def backward_kernel(
-    owner_rows, hidden_ref, turned_ref, cot_ref, head_ref, part_ref,
-    grads, view, head_big, head_sum, bias_sum,
+    owner_rows, hidden_in, turned_in, cot_ref, head_ref, part_ref,
+    hidden_ref, turned_ref, grads, view, head_big, head_sum, bias_sum, hidden_sem, turned_sem,
 ):
+    def fetch(pair):
+        rows = pl.ds(pl.multiple_of(pair * 2 * COARSE, 2 * COARSE), 2 * COARSE)
+        return pltpu.make_async_copy(
+            hidden_in.at[rows, :], hidden_ref.at[rows, :], hidden_sem.at[pair]
+        )
+
+    @pl.loop(0, hidden_ref.shape[0] // (2 * COARSE))
+    def _(pair):
+        fetch(pair).start()
+
+    fetch_turned = pltpu.make_async_copy(turned_in, turned_ref, turned_sem)
+    fetch_turned.start()
     slots = hidden_ref.shape[0] // COARSE
     half = hidden_ref.shape[1] // 2
     c_out = half // 4
@@ -132,6 +161,7 @@
     @pl.loop(0, slots // 2)
     def _(pair):
         rows = pl.ds(pl.multiple_of(pair * 2 * COARSE, 2 * COARSE), 2 * COARSE)
+        fetch(pair).wait()
         here = view[...].astype(jnp.float32)
         here = jnp.concatenate([here, here], axis=0)
         here = jnp.where(lane_slot == row_slot + 2 * pair, here, 0.0).astype(bf)
@@ -149,6 +179,7 @@
             rest = (active - top.astype(jnp.float32)).astype(bf)
             head_sum[...] += dot(mine, jnp.concatenate([top, rest], axis=1), ((0,), (0,)))
 
+    fetch_turned.wait()
     for s in range(8):
         for h in range(2):
             if s >= 4 and h == 0:
@@ -290,14 +321,19 @@
     return pl.pallas_call(
         forward_kernel,
         out_shape=(
-            jax.ShapeDtypeStruct((slots * COARSE, 8 * c_out), jnp.float32),
-            jax.ShapeDtypeStruct((8, c_in, slots * COARSE), jnp.bfloat16),
+            pltpu.HBM((slots * COARSE, 8 * c_out), jnp.float32),
+            pltpu.HBM((8, c_in, slots * COARSE), jnp.bfloat16),
         ),
+        out_specs=(pl.BlockSpec(memory_space=pltpu.HBM),) * 2,
         scratch_shapes=[
+            pltpu.VMEM((slots * COARSE, 8 * c_out), jnp.float32),
+            pltpu.VMEM((8, c_in, slots * COARSE), jnp.bfloat16),
             pltpu.VMEM((slots * CELLS_UP, c_in), jnp.bfloat16),
             pltpu.VMEM((8 * c_in, 8 * c_out), jnp.bfloat16),
             pltpu.VMEM((16 * COARSE, 2 * CELLS_UP), jnp.bfloat16),
             pltpu.VMEM((2 * CELLS_UP, 16 * COARSE), jnp.bfloat16),
+            pltpu.SemaphoreType.DMA((slots // 2,)),
+            pltpu.SemaphoreType.DMA((slots // 2,)),
         ],
         compiler_params=LIMIT,
         cost_estimate=pl.CostEstimate(
@@ -317,14 +353,20 @@
     return pl.pallas_call(
         functools.partial(backward_kernel, owner_rows),
         out_shape=jax.ShapeDtypeStruct((c_in, blocks * c_out), jnp.float32),
+        in_specs=[pl.BlockSpec(memory_space=pltpu.HBM)] * 2
+        + [pl.BlockSpec(memory_space=pltpu.VMEM)] * 2,
         scratch_shapes=[
+            pltpu.VMEM((slots * COARSE, 8 * c_out), jnp.float32),
+            pltpu.VMEM((8, c_in, slots * COARSE), jnp.bfloat16),
             pltpu.VMEM((slots * COARSE, 8 * c_out), jnp.bfloat16),
             pltpu.VMEM((COARSE, 8 * group), jnp.bfloat16),
             pltpu.VMEM((12 * group, 4 * c_out), jnp.bfloat16),
             pltpu.VMEM((4 * group, 8 * c_out), jnp.float32),
             pltpu.VMEM((1, 8 * c_out), jnp.float32),
+            pltpu.SemaphoreType.DMA((slots // 2,)),
+            pltpu.SemaphoreType.DMA,
         ],
-        compiler_params=LIMIT,
+        compiler_params=pltpu.CompilerParams(vmem_limit_bytes=61 * 1024 * 1024),
         cost_estimate=pl.CostEstimate(
             flops=8 * slots * COARSE * TAPS * c_in * c_out,
             bytes_accessed=8 * 1024 * 1024,

time: 61.3 us -> 60.3 us (0.984)
  local copies, waits for them, and re-layouts: 15.5 us -> 11.3 us
  Pallas kernels: 29.8 us -> 33.1 us
    unnamed x14 -> x8, local copies, waits for them, and re-layouts: 9.75 us -> 4.27 us
    pallas_call x1, Pallas kernels: 6.13 us -> 8.65 us  [backward(): pl.pallas_call(functools.partial(backward_kernel, owner_rows), out_shape=...]
    pallas_call x1, Pallas kernels: 7.08 us -> 8.03 us  [forward(): pl.pallas_call(forward_kernel, out_shape=(pltpu.HBM((slots * COARSE, 8 *...]
    reshape x1, local copies, waits for them, and re-layouts: 0.02 us -> 0.65 us  [backward(): work_cot.reshape(group, FINE)]
  transfers between devices with their start and end apart: 2 -> 2, of which waited for: 0 -> 0; matrix products, arithmetic and copies ran while one was open for 7% -> 8% of each run, Pallas kernels for 12% -> 13%
where the time goes in v4:
time: 60.3 us; the launch traced here: 59.9 us
  Pallas kernels  33.1 us (55%)
  starting transfers between devices  12.6 us (21%)
  local copies, waits for them, and re-layouts  11.3 us (19%)
  other arithmetic  2.27 us (4%)
  between operations  0.76 us (1%)
    pallas_call x1, Pallas kernels, add_up(): pl.pallas_call(functools.partial(reduce_kernel, c_out, scale), out_shape=...  16.4 us
    pallas_call x1, Pallas kernels, backward(): pl.pallas_call(functools.partial(backward_kernel, owner_rows), out_shape=...  8.65 us
    pallas_call x1, Pallas kernels, forward(): pl.pallas_call(forward_kernel, out_shape=(pltpu.HBM((slots * COARSE, 8 *...  8.03 us
    all_to_all x1, starting transfers between devices, on_device(): incoming = exchange(jnp.sum(hits, axis=0))  6.55 us
    all_to_all x1, starting transfers between devices, on_device(): arrived = exchange(outgoing.reshape(owners, per_pair, FIELDS, FINE))  6.02 us
    unnamed x8, local copies, waits for them, and re-layouts  4.27 us
    another operation x2, local copies, waits for them, and re-layouts, backward(): jnp.tile(head_weight.T, (1, 4))  1.36 us
    gather x1, local copies, waits for them, and re-layouts, on_device(): outgoing = cotangent[jnp.minimum(slot_place, train_rows - 1)]  1.31 us
  transfers between devices with their start and end apart: 2, of which 0 were waited for; matrix products, arithmetic and copies ran while one was open for 8% of the time, Pallas kernels for 13%

profile of v4, /device:TPU:13, one launch (start us, length us, event | category | flops | bytes accessed | tf_op | source)
XLA Modules:
  0.0 59.9 jit_solution(1116018658496742440)
XLA Ops:
  0.6 0.0 copy-start
  0.6 0.0 copy-start.2
  0.7 1.0 %convert_reduce_fusion = (s32[16]{0:T(128)S(1)}, s32[16]{0:T(128)S(1)}) fusion(s32[16]{0:T(128)} %param.7), kind=kLoop, calls=%fused_computation.2 | loop fusion | flops 2016 | bytes 192 | tf_op jit(solution)/shard_map/reduce_sum | solution.py:393
  1.6 0.7 %copy.23 = s32[16,1,1]{2,1,0:T(1,128)} copy(s32[16,1,1]{0,2,1:T(1,128)S(1)} %bitcast.18) | data formatting | bytes 128 | tf_op jit(solution)/shard_map/all_to_all | solution.py:391
  2.3 6.6 %all-to-all-start = ((s32[16,1,1]{2,1,0:T(1,128)}), s32[16,1,1]{2,1,0:T(1,128)S(1)}, u32[]{:S(2)}, u32[]{:S(2)}) async-start(s32[16,1,1]{2,1,0:T(1,128)} %copy.23), calls=%async_computation | async-start | bytes 16384 | tf_op jit(solution)/shard_map/all_to_all | solution.py:391
  8.9 0.7 %compare_select_fusion = s32[16]{0:T(128)S(1)} fusion(s32[16]{0:T(128)S(1)} %get-tuple-element.26, s32[16]{0:T(128)} %param.7), kind=kLoop, calls=%fused_computation.12 | loop fusion | flops 80 | bytes 192 | tf_op jit(solution)/shard_map/select_n | solution.py:405
  9.5 0.7 %tile.8 = f32[8,64]{1,0:T(8,128)S(1)} broadcast(f32[64]{0:T(128)} %param.10), dimensions={1} | broadcast | bytes 2304 | tf_op jit(solution)/shard_map/tile | solution.py:344
  10.2 0.1 tile.18.bias_ref
  10.3 0.7 %tile.19 = f32[4,4,64]{2,1,0:T(4,128)S(1)} broadcast(f32[4,64]{1,0:T(4,128)} %bitcast.17), dimensions={0,2} | broadcast | bytes 5120 | tf_op jit(solution)/shard_map/tile | solution.py:375
  10.9 0.7 %tile.20.head_ref = f32[4,256]{1,0:T(4,128)} reshape(f32[4,4,64]{2,1,0:T(4,128)S(1)} %tile.19) | data formatting | bytes 8192 | tf_op jit(solution)/shard_map/tile | solution.py:375
  11.6 2.0 %copy.24 = bf16[256,27,64]{2,0,1:T(8,128)(2,1)S(1)} copy(bf16[256,27,64]{0,2,1:T(8,128)(2,1)} %param.9) | data formatting | bytes 1769472 | tf_op args[3]
  13.6 0.0 all-to-all-done
  13.6 0.4 reduce
  14.0 0.1 select_reduce_fusion
  14.1 0.1 add_minimum_fusion
  14.2 0.1 min.18
  14.3 1.3 %gather_fusion = bf16[32,4,512]{2,1,0:T(4,128)(2,1)} fusion(bf16[32,4,512]{2,1,0:T(4,128)(2,1)S(1)} %copy-done, s32[1024]{0:T(1024)S(1)} %pad_clamp_fusion.1), kind=kCustom, calls=%fused_computation | custom fusion | bytes 262272 | tf_op jit(solution)/shard_map/gather | solution.py:400
  15.6 6.0 %all-to-all-start.1 = ((bf16[16,2,4,512]{3,2,1,0:T(4,128)(2,1)}), bf16[16,2,4,512]{3,2,1,0:T(4,128)(2,1)S(1)}, u32[]{:S(2)}, u32[]{:S(2)}) async-start(bf16[16,2,4,512]{3,2,1,0:T(4,128)(2,1)} %bitcast.3), calls=%async_computation.1 | async-start | bytes 262144 | tf_op jit(solution)/shard_map/all_to_all | solution.py:402
  21.6 0.3 copy.25.patch_ref
  22.0 8.0 %shard_map.85 = (f32[1024,512]{1,0:T(8,128)}, bf16[8,256,1024]{2,1,0:T(8,128)(2,1)}) custom-call(bf16[16,125,256]{2,1,0:T(8,128)(2,1)S(1)} %copy.25.patch_ref, bf16[27,256,64]{2,1,0:T(8,128)(2,1)S(1)} %bitcast.14, f32[1,512]{1,0:T(1,128)S(1)} %tile.18.bias_ref), custom_call_target="tpu_custom_call" | custom-call | flops 3623878656 | bytes 10485760 | tf_op jit(solution)/shard_map/pallas_call | solution.py:321
  30.0 0.0 all-to-all-done.1
  30.0 0.6 %gather_fusion.1 = bf16[16,4,512]{2,1,0:T(4,128)(2,1)S(1)} fusion(bf16[32,4,512]{2,1,0:T(4,128)(2,1)S(1)} %bitcast.16, s32[1024]{0:T(1024)S(1)} %pad_clamp_fusion), kind=kCustom, calls=%fused_computation.1 | custom fusion | bytes 131136 | tf_op jit(solution)/shard_map/gather | solution.py:405
  30.6 0.7 %reshape.75.cot_ref = bf16[64,512]{1,0:T(8,128)(2,1)} reshape(bf16[16,4,512]{2,1,0:T(4,128)(2,1)S(1)} %gather_fusion.1) | data formatting | bytes 131072 | tf_op jit(solution)/shard_map/reshape | solution.py:375
  31.3 8.7 %shard_map.86 = f32[256,1792]{1,0:T(8,128)} custom-call(f32[1024,512]{1,0:T(8,128)} %get-tuple-element.8.hidden_in, bf16[8,256,1024]{2,1,0:T(8,128)(2,1)} %get-tuple-element.9.turned_in, bf16[64,512]{1,0:T(8,128)(2,1)} %reshape.75.cot_ref, f32[4,256]{1,0:T(4,128)} %tile.20.head_ref), custom_call_target="tpu_custom_call" | custom-call | flops 3623878656 | bytes 8388608 | tf_op jit(solution)/shard_map/pallas_call | solution.py:353
  40.0 0.0 copy-start.1
  40.0 1.5 %copy-done.1 = f32[256,1792]{1,0:T(8,128)S(1)} copy-done((f32[256,1792]{1,0:T(8,128)S(1)}, f32[256,1792]{1,0:T(8,128)}, u32[]{:S(2)}) %copy-start.1) | copy-done | bytes 1835032
  41.5 16.4 %shard_map.87 = f32[16,1792]{1,0:T(8,128)S(1)} custom-call(f32[8,2,16,1792]{3,2,1,0:T(8,128)S(1)} %bitcast.13), custom_call_target="tpu_custom_call" | custom-call | tf_op jit(solution)/shard_map/pallas_call | solution.py:298
  57.8 0.1 slice_add_fusion
  57.9 0.5 slice_bitcast_fusion.1
  58.4 0.6 slice_bitcast_fusion
  59.0 0.1 reshape.77
  59.1 0.8 %copy.26 = f32[16,27,64]{2,0,1:T(8,128)} copy(f32[16,27,64]{2,1,0:T(8,128)S(1)} %reshape.77) | data formatting | bytes 221184
  (5 shorter events, 0.0 us)
Async XLA Ops:
  0.6 13.7 %copy-start = (bf16[32,4,512]{2,1,0:T(4,128)(2,1)S(1)}, bf16[32,4,512]{2,1,0:T(4,128)(2,1)}, u32[]{:S(2)}) copy-start(bf16[32,4,512]{2,1,0:T(4,128)(2,1)} %param.8) | copy-start | bytes 393220
  0.6 21.0 %copy-start.2 = (bf16[16,125,256]{2,0,1:T(8,128)(2,1)S(1)}, bf16[16,125,256]{2,0,1:T(8,128)(2,1)}, u32[]{:S(2)}) copy-start(bf16[16,125,256]{2,0,1:T(8,128)(2,1)} %param.6) | copy-start | bytes 3072004
  2.3 11.3 %all-to-all-start = ((s32[16,1,1]{2,1,0:T(1,128)}), s32[16,1,1]{2,1,0:T(1,128)S(1)}, u32[]{:S(2)}, u32[]{:S(2)}) async-start(s32[16,1,1]{2,1,0:T(1,128)} %copy.23), calls=%async_computation | async-start | bytes 16384 | tf_op jit(solution)/shard_map/all_to_all | solution.py:391
  15.6 14.4 %all-to-all-start.1 = ((bf16[16,2,4,512]{3,2,1,0:T(4,128)(2,1)}), bf16[16,2,4,512]{3,2,1,0:T(4,128)(2,1)S(1)}, u32[]{:S(2)}, u32[]{:S(2)}) async-start(bf16[16,2,4,512]{3,2,1,0:T(4,128)(2,1)} %bitcast.3), calls=%async_computation.1 | async-start | bytes 262144 | tf_op jit(solution)/shard_map/all_to_all | solution.py:402
  40.0 1.5 %copy-start.1 = (f32[256,1792]{1,0:T(8,128)S(1)}, f32[256,1792]{1,0:T(8,128)}, u32[]{:S(2)}) copy-start(f32[256,1792]{1,0:T(8,128)} %shard_map.86) | copy-start | bytes 5505028
